TPU v7x, 32 devices: a whole 2x2x4 slice. The times are simulated.
32 devices in a mesh: gx: 4 (over z), gy: 4 (over y, x), gz: 2 (over core).
Axes of the slice: x: 2, y: 2, z: 4, core: 2. Of those that a mesh axis runs over, the one named last changes fastest.
Arguments:
- populations0: bfloat16 [26, 16, 32, 512], P(None, 'gz', 'gx', 'gy'), may hold values from 0 to 1, as said below
- populations1: bfloat16 [26, 16, 32, 512], P(None, 'gz', 'gx', 'gy'), may hold values from 0 to 1, as said below
- cotangent: float32 [26, 16, 32, 512], P(None, 'gz', 'gx', 'gy'), may hold values from -6 to 6
Outputs:
- gradient: float32 [26, 16, 32, 512], P(None, 'gz', 'gx', 'gy')
Inputs may be any that keep to these rules, and one draw needn't show every extreme that they name: `populations0`: every entry is positive; in every cell the 7 phase populations sum to between 0.1 and 1.3. `populations1`: every entry is positive; in every cell the 7 phase populations sum to between 0.1 and 1.3.
All inputs are finite; a program needn't handle non-finite values.
Results may differ from a plain program's by a relative error of at most 0.0003.
Values sent between devices are 32-bit elements; how exact they have to be, the bound alone decides.
A program may use at most 64 MiB of HBM per device.

v0:
```python
import jax
import jax.numpy as jnp
import numpy as np
from jax import lax
from jax.sharding import PartitionSpec as P

VELOCITY = np.array(
    [
        [0, 0, 0],
        [1, 0, 0],
        [-1, 0, 0],
        [0, 1, 0],
        [0, -1, 0],
        [0, 0, 1],
        [0, 0, -1],
        [1, 1, 0],
        [-1, -1, 0],
        [1, -1, 0],
        [-1, 1, 0],
        [1, 0, 1],
        [-1, 0, -1],
        [1, 0, -1],
        [-1, 0, 1],
        [0, 1, 1],
        [0, -1, -1],
        [0, 1, -1],
        [0, -1, 1],
    ]
)
OPPOSITE = [0, 2, 1, 4, 3, 6, 5, 8, 7, 10, 9, 12, 11, 14, 13, 16, 15, 18, 17]
FLOW_WEIGHT = [1.0 / 3.0] + [1.0 / 18.0] * 6 + [1.0 / 36.0] * 12
PHASE_WEIGHT = [0.25] + [0.125] * 6
VELOCITY_ALL = np.concatenate([VELOCITY, VELOCITY[:7]], 0)
OPPOSITE_ALL = OPPOSITE + [19 + mirror for mirror in OPPOSITE[:7]]
WELL_DEPTH = 0.3
STIFFNESS = 0.6
SHARPEN = 0.3
PHASE_RATE = 1.4
UNITS = ((1, 0, 0), (0, 1, 0), (0, 0, 1))
CENTER = (0, 0, 0)


def extended_2(shard, sides, width):
    for axis, dim in sides:
        count, length = (lax.axis_size(axis), shard.shape[dim])
        up = [(i, (i + 1) % count) for i in range(count)]
        down = [(j, i) for i, j in up]
        last = lax.slice_in_dim(shard, length - width, length, axis=dim)
        first = lax.slice_in_dim(shard, 0, width, axis=dim)
        before = lax.ppermute(last, axis, up)
        after = lax.ppermute(first, axis, down)
        shard = jnp.concatenate([before, shard, after], axis=dim)
    return shard


def expand(weights, rank):
    values = [float(entry) for entry in list(weights)]
    return jnp.asarray(values, jnp.float32).reshape((-1,) + (1,) * rank)


def along(velocity_table, vector):
    rank = vector.ndim - 1
    total = expand(velocity_table[:, 0], rank) * vector[0]
    for direction in range(1, 3):
        total = total + expand(velocity_table[:, direction], rank) * vector[direction]
    return total


def collide(populations, phase_grad, potential_grad):
    rank = populations.ndim - 1
    flow_part = populations[:19]
    phase_part = populations[19:]
    fraction = jnp.sum(phase_part, 0)
    density = 0.2 + 0.8 * fraction
    pressure = jnp.sum(flow_part, 0)
    body_force = -fraction[None] * potential_grad
    momentum = jnp.stack(
        [jnp.sum(expand(VELOCITY[:, direction], rank) * flow_part, 0) for direction in range(3)]
    )
    velocity = (momentum + 0.5 * body_force) / density[None]
    along_flow = along(VELOCITY, velocity)
    speed_square = jnp.sum(velocity * velocity, 0)
    relax_rate = 1.1 + 0.5 * fraction
    flow_equil = expand(FLOW_WEIGHT, rank) * (
        pressure + density * (3.0 * along_flow + 4.5 * along_flow * along_flow - 1.5 * speed_square)
    )
    along_force = along(VELOCITY, body_force)
    speed_force = jnp.sum(velocity * body_force, 0)
    source = expand(FLOW_WEIGHT, rank) * (
        3.0 * (along_force - speed_force) + 9.0 * along_flow * along_force
    )
    flow_post = (
        flow_part - relax_rate * (flow_part - flow_equil) + (1.0 - 0.5 * relax_rate) * source
    )
    magnitude = jnp.sqrt(jnp.sum(phase_grad * phase_grad, 0) + 0.0625)
    normal = phase_grad / magnitude
    along_normal = along(VELOCITY[:7], normal)
    phase_equil = expand(PHASE_WEIGHT, rank) * (
        fraction * (1.0 + 4.0 * along_flow[:7])
        + 4.0 * SHARPEN * fraction * (1.0 - fraction) * along_normal
    )
    phase_post = phase_part - PHASE_RATE * (phase_part - phase_equil)
    return jnp.concatenate([flow_post, phase_post], 0)


def wall_zero(extended, width, vertical_dim):
    height = extended.shape[vertical_dim]
    layer_index = lax.broadcasted_iota(jnp.int32, (height,), 0)
    position = lax.axis_index("gz")
    bricks = lax.axis_size("gz")
    bottom_wall = jnp.logical_and(layer_index < width, position == 0)
    top_wall = jnp.logical_and(layer_index >= height - width, position == bricks - 1)
    inside = jnp.where(jnp.logical_or(bottom_wall, top_wall), 0.0, 1.0).astype(extended.dtype)
    extent = [1] * extended.ndim
    extent[vertical_dim] = height
    return extended * inside.reshape(extent)


def offset_view(extended, margin, offset, extent):
    return extended[
        ...,
        margin + offset[0] : margin + offset[0] + extent[0],
        margin + offset[1] : margin + offset[1] + extent[1],
        margin + offset[2] : margin + offset[2] + extent[2],
    ]


def negate(offset):
    return tuple((-entry for entry in offset))


def gradient(extended, margin, extent):
    return jnp.stack(
        [
            (
                offset_view(extended, margin, unit, extent)
                - offset_view(extended, margin, negate(unit), extent)
            )
            * 0.5
            for unit in UNITS
        ]
    )


def laplace(extended, margin, extent):
    total = -6.0 * offset_view(extended, margin, CENTER, extent)
    for unit in UNITS:
        total = (
            total
            + offset_view(extended, margin, unit, extent)
            + offset_view(extended, margin, negate(unit), extent)
        )
    return total


def spread(extended, margin, extent):
    total = jnp.zeros(extent, jnp.float32)
    for direction in range(3):
        unit = UNITS[direction]
        total = (
            total
            + (
                offset_view(extended[direction], margin, negate(unit), extent)
                - offset_view(extended[direction], margin, unit, extent)
            )
            * 0.5
        )
    return total


def well_term(fraction):
    return 4.0 * WELL_DEPTH * fraction * (fraction - 1.0) * (fraction - 0.5)


def well_slope(fraction):
    return 4.0 * WELL_DEPTH * (3.0 * fraction * fraction - 3.0 * fraction + 0.5)


def bounce(arrived, adjoint):
    height = adjoint.shape[1]
    layer_index = lax.broadcasted_iota(jnp.int32, (height,), 0)
    position = lax.axis_index("gz")
    bricks = lax.axis_size("gz")
    bottom_wall = jnp.logical_and(layer_index == 0, position == 0).reshape((1, height, 1, 1))
    top_wall = jnp.logical_and(layer_index == height - 1, position == bricks - 1).reshape(
        (1, height, 1, 1)
    )
    rising = jnp.asarray((VELOCITY_ALL[:, 0] == 1).reshape((26, 1, 1, 1)))
    falling = jnp.asarray((VELOCITY_ALL[:, 0] == -1).reshape((26, 1, 1, 1)))
    reflect = jnp.logical_or(
        jnp.logical_and(rising, top_wall), jnp.logical_and(falling, bottom_wall)
    )
    flipped = jnp.stack([adjoint[mirror] for mirror in OPPOSITE_ALL])
    return jnp.where(reflect, flipped, arrived)


def stream_adjoint(adjoint, extent):
    extended = extended_2(adjoint, (("gx", 2), ("gy", 3), ("gz", 1)), 1)
    arrived = jnp.stack(
        [
            offset_view(
                extended[member], 1, tuple((int(entry) for entry in VELOCITY_ALL[member])), extent
            )
            for member in range(26)
        ]
    )
    return bounce(arrived, adjoint)


def adjoint_step(stored, adjoint):
    populations = stored.astype(jnp.float32)
    fraction = jnp.sum(populations[19:], 0)
    extent = fraction.shape
    extended = wall_zero(extended_2(fraction, (("gx", 1), ("gy", 2), ("gz", 0)), 2), 2, 0)
    larger = tuple((entry + 2 for entry in extent))
    potential_ext = well_term(offset_view(extended, 1, CENTER, larger)) - STIFFNESS * laplace(
        extended, 1, larger
    )
    potential_ext = wall_zero(potential_ext, 1, 0)
    phase_grad = gradient(extended, 2, extent)
    potential_grad = gradient(potential_ext, 1, extent)
    arrived = stream_adjoint(adjoint, extent)
    pullback = jax.vjp(collide, populations, phase_grad, potential_grad)[1]
    adjoint_pops, adjoint_pgrad, adjoint_mgrad = pullback(arrived)
    combined = jnp.concatenate([adjoint_pgrad, adjoint_mgrad], 0)
    wide_ext = wall_zero(extended_2(combined, (("gx", 2), ("gy", 3), ("gz", 1)), 2), 2, 1)
    larger = tuple((entry + 2 for entry in extent))
    adjoint_mu_ext = wall_zero(spread(wide_ext[3:], 1, larger), 1, 0)
    adjoint_mu = offset_view(adjoint_mu_ext, 1, CENTER, extent)
    adjoint_phase = (
        well_slope(fraction) * adjoint_mu
        - STIFFNESS * laplace(adjoint_mu_ext, 1, extent)
        + spread(wide_ext[:3], 2, extent)
    )
    return jnp.concatenate([adjoint_pops[:19], adjoint_pops[19:] + adjoint_phase[None]], 0)


def local(populations0, populations1, cotangent):
    adjoint1 = adjoint_step(populations1, cotangent)
    return adjoint_step(populations0, adjoint1)


def solution(mesh):
    return jax.shard_map(
        local,
        mesh=mesh,
        in_specs=(P(None, "gz", "gx", "gy"), P(None, "gz", "gx", "gy"), P(None, "gz", "gx", "gy")),
        out_specs=P(None, "gz", "gx", "gy"),
        check_vma=False,
    )
```

profile of v0, /device:TPU:0, one launch (start us, length us, event | category | flops | bytes accessed | tf_op | source)
XLA Modules:
  0.0 186.3 jit_solution(9328866406122782875)
XLA Ops:
  0.0 2.3 %fusion.76 = (f32[26,8,1,128]{3,2,1,0:T(1,128)}, f32[26,8,1,128]{3,2,1,0:T(1,128)}) fusion(f32[26,8,8,128]{3,2,1,0:T(8,128)} %param.39), kind=kLoop, calls=%fused_computation.555 | loop fusion | bytes 425984 | tf_op jit(solution)/shard_map/slice | solution.py:48
  2.3 5.0 %collective-permute-start.1 = (f32[26,8,1,128]{3,2,1,0:T(1,128)}, f32[26,8,1,128]{3,2,1,0:T(1,128)S(1)}, u32[]{:S(2)}, u32[]{:S(2)}) collective-permute-start(f32[26,8,1,128]{3,2,1,0:T(1,128)} %get-tuple-element.168), channel_id=1, source_target_pairs={{8,0},{16,8},{24,16},{0,24},{9,1},{17,9},{25,17},{1,25},{10,2},{18... | collective-permute-start | bytes 319496 | tf_op jit(solution)/shard_map/ppermute | solution.py:51
  10.8 2.3 %collective-permute-start.7 = (f32[8,2,128]{2,1,0:T(2,128)S(1)}, f32[8,2,128]{2,1,0:T(2,128)S(1)}, u32[]{:S(2)}, u32[]{:S(2)}) collective-permute-start(f32[8,2,128]{2,1,0:T(2,128)S(1)} %get-tuple-element.246), channel_id=1, source_target_pairs={{8,0},{16,8},{24,16},{0,24},{9,1},{17,9},{25,17},{1,25},{10,2},{18... | collective-permute-start | bytes 24584 | tf_op jit(solution)/shard_map/ppermute | solution.py:51
  32.1 2.5 %collective-permute-start.27 = (f32[8,12,2]{2,1,0:T(8,128)S(1)}, f32[8,12,2]{2,1,0:T(8,128)S(1)}, u32[]{:S(2)}, u32[]{:S(2)}) collective-permute-start(f32[8,12,2]{2,1,0:T(8,128)S(1)} %get-tuple-element.224), channel_id=1, source_target_pairs={{2,0},{4,2},{6,4},{0,6},{3,1},{5,3},{7,5},{1,7},{10,8},{12,10},{14... | collective-permute-start | bytes 2312 | tf_op jit(solution)/shard_map/ppermute | solution.py:51
  34.7 2.9 %collective-permute-start.9 = (f32[8,12,2]{2,1,0:T(8,128)S(1)}, f32[8,12,2]{2,1,0:T(8,128)S(1)}, u32[]{:S(2)}, u32[]{:S(2)}) collective-permute-start(f32[8,12,2]{2,1,0:T(8,128)S(1)} %get-tuple-element.226), channel_id=1, source_target_pairs={{2,0},{4,2},{6,4},{0,6},{3,1},{5,3},{7,5},{1,7},{10,8},{12,10},{14... | collective-permute-start | bytes 2312 | tf_op jit(solution)/shard_map/ppermute | solution.py:51
  37.6 2.8 %collective-permute-done.26 = f32[8,12,2]{2,1,0:T(8,128)S(1)} collective-permute-done((f32[8,12,2]{2,1,0:T(8,128)S(1)}, f32[8,12,2]{2,1,0:T(8,128)S(1)}, u32[]{:S(2)}, u32[]{:S(2)}) %collective-permute-start.26) | collective-permute-done | bytes 800 | tf_op jit(solution)/shard_map/ppermute | solution.py:50
  51.9 1.8 fusion.75
  53.8 2.8 %copy.117 = f32[26,8,10,1]{0,1,3,2:T(8,128)} copy(f32[26,8,10,1]{3,2,1,0:T(8,128)} %get-tuple-element.136) | data formatting | bytes 16640 | tf_op jit(solution)/shard_map/slice | solution.py:49
  58.1 2.0 %collective-permute-start.2 = (f32[26,8,10,1]{0,1,3,2:T(8,128)}, f32[26,8,10,1]{0,1,3,2:T(8,128)}, u32[]{:S(2)}, u32[]{:S(2)}) collective-permute-start(f32[26,8,10,1]{0,1,3,2:T(8,128)} %copy.116), channel_id=1, source_target_pairs={{0,2},{2,4},{4,6},{6,0},{1,3},{3,5},{5,7},{7,1},{8,10},{10,12},{12... | collective-permute-start | bytes 24968 | tf_op jit(solution)/shard_map/ppermute | solution.py:50
  61.6 2.4 %copy.119 = f32[26,8,10,1]{3,2,1,0:T(8,128)S(1)} copy(f32[26,8,10,1]{0,1,3,2:T(8,128)} %collective-permute-done.3) | data formatting | bytes 16640 | tf_op jit(solution)/shard_map/ppermute | solution.py:51
  63.9 3.4 %copy.118 = f32[26,8,10,1]{3,2,1,0:T(8,128)} copy(f32[26,8,10,1]{0,1,3,2:T(8,128)} %collective-permute-done.2) | data formatting | bytes 16640 | tf_op jit(solution)/shard_map/ppermute | solution.py:50
  71.6 3.1 %pad_maximum_fusion = f32[26,10,10,130]{3,2,1,0:T(8,128)S(1)} fusion(f32[26,1,10,130]{3,2,1,0:T(8,128)S(1)} %collective-permute-done.5, f32[26,8,10,1]{3,2,1,0:T(8,128)S(1)} %copy.119, f32[26,8,1,128]{3,2,1,0:T(1,128)S(1)} %copy-done.8, f32[26,8,8,128]{3,2,1,0:T(8,128)S(1)} %copy-done, f32[26,8,1,128]{3,2,1,0:T(1,128)S(1)} %copy-done.10, ...), kind=kLoop, calls=%fused_computation | loop fusion | flops 2028000 | bytes 2704000 | tf_op jit(solution)/shard_map/concatenate | solution.py:52
  86.7 3.7 %collective-permute-start.13 = (f32[6,8,2,128]{3,2,1,0:T(2,128)S(1)}, f32[6,8,2,128]{3,2,1,0:T(2,128)S(1)}, u32[]{:S(2)}, u32[]{:S(2)}) collective-permute-start(f32[6,8,2,128]{3,2,1,0:T(2,128)S(1)} %get-tuple-element.185), channel_id=1, source_target_pairs={{8,0},{16,8},{24,16},{0,24},{9,1},{17,9},{25,17},{1,25},{10,2},{18... | collective-permute-start | bytes 147464 | tf_op jit(solution)/shard_map/ppermute | solution.py:51
  92.2 4.1 %collective-permute-done.12 = f32[6,8,2,128]{3,2,1,0:T(2,128)S(1)} collective-permute-done((f32[6,8,2,128]{3,2,1,0:T(2,128)S(1)}, f32[6,8,2,128]{3,2,1,0:T(2,128)S(1)}, u32[]{:S(2)}, u32[]{:S(2)}) %collective-permute-start.12) | collective-permute-done | bytes 49184 | tf_op jit(solution)/shard_map/ppermute | solution.py:50
  98.6 10.0 %collective-permute-done.15 = f32[6,8,12,2]{3,2,1,0:T(8,128)S(1)} collective-permute-done((f32[6,8,12,2]{3,2,1,0:T(8,128)S(1)}, f32[6,8,12,2]{3,2,1,0:T(8,128)S(1)}, u32[]{:S(2)}, u32[]{:S(2)}) %collective-permute-start.15) | collective-permute-done | bytes 4640 | tf_op jit(solution)/shard_map/ppermute | solution.py:51
  108.6 6.1 %collective-permute-done.14 = f32[6,8,12,2]{3,2,1,0:T(8,128)S(1)} collective-permute-done((f32[6,8,12,2]{3,2,1,0:T(8,128)S(1)}, f32[6,8,12,2]{3,2,1,0:T(8,128)S(1)}, u32[]{:S(2)}, u32[]{:S(2)}) %collective-permute-start.14) | collective-permute-done | bytes 4640 | tf_op jit(solution)/shard_map/ppermute | solution.py:50
  120.9 5.4 %collective-permute-done.19 = f32[26,8,1,128]{3,1,2,0:T(8,128)S(1)} collective-permute-done((f32[26,8,1,128]{3,1,2,0:T(8,128)S(1)}, f32[26,8,1,128]{3,1,2,0:T(8,128)S(1)}, u32[]{:S(2)}, u32[]{:S(2)}) %collective-permute-start.19) | collective-permute-done | bytes 106528 | tf_op jit(solution)/shard_map/ppermute | solution.py:51
  128.4 2.8 %copy.125 = f32[26,8,10,1]{0,1,3,2:T(8,128)} copy(f32[26,8,10,1]{3,2,1,0:T(8,128)} %get-tuple-element.134) | data formatting | bytes 16640 | tf_op jit(solution)/shard_map/slice | solution.py:49
  135.5 2.4 %copy.127 = f32[26,8,10,1]{3,2,1,0:T(8,128)S(1)} copy(f32[26,8,10,1]{0,1,3,2:T(8,128)} %collective-permute-done.21) | data formatting | bytes 16640 | tf_op jit(solution)/shard_map/ppermute | solution.py:51
  139.5 3.4 %copy.126 = f32[26,8,10,1]{3,2,1,0:T(8,128)} copy(f32[26,8,10,1]{0,1,3,2:T(8,128)} %collective-permute-done.20) | data formatting | bytes 16640 | tf_op jit(solution)/shard_map/ppermute | solution.py:50
  147.1 4.0 %pad_maximum_fusion.1 = f32[26,10,10,130]{3,2,1,0:T(8,128)S(1)} fusion(f32[26,1,10,130]{3,2,1,0:T(8,128)S(1)} %collective-permute-done.23, f32[26,8,10,1]{3,2,1,0:T(8,128)S(1)} %copy.127, f32[26,8,1,128]{3,2,1,0:T(1,128)S(1)} %bitcast.438, f32[7,8,8,128]{3,2,1,0:T(8,128)S(1)} %add_add_fusion.2, f32[19,8,8,128]{3,2,1,0:T(8,128)S(1)} %pad_add_fusion, ...), kind=kLoop, calls=%fused_computation.1 | loop fusion | flops 2366000 | bytes 2704000 | tf_op jit(solution)/shard_map/concatenate | solution.py:52
  160.4 2.4 %collective-permute-done.30 = f32[6,8,2,128]{3,2,1,0:T(2,128)S(1)} collective-permute-done((f32[6,8,2,128]{3,2,1,0:T(2,128)S(1)}, f32[6,8,2,128]{3,2,1,0:T(2,128)S(1)}, u32[]{:S(2)}, u32[]{:S(2)}) %collective-permute-start.30) | collective-permute-done | bytes 49184 | tf_op jit(solution)/shard_map/ppermute | solution.py:50
  165.2 10.0 %collective-permute-done.33 = f32[6,8,12,2]{3,2,1,0:T(8,128)S(1)} collective-permute-done((f32[6,8,12,2]{3,2,1,0:T(8,128)S(1)}, f32[6,8,12,2]{3,2,1,0:T(8,128)S(1)}, u32[]{:S(2)}, u32[]{:S(2)}) %collective-permute-start.33) | collective-permute-done | bytes 4640 | tf_op jit(solution)/shard_map/ppermute | solution.py:51
  175.2 6.3 %collective-permute-done.32 = f32[6,8,12,2]{3,2,1,0:T(8,128)S(1)} collective-permute-done((f32[6,8,12,2]{3,2,1,0:T(8,128)S(1)}, f32[6,8,12,2]{3,2,1,0:T(8,128)S(1)}, u32[]{:S(2)}, u32[]{:S(2)}) %collective-permute-start.32) | collective-permute-done | bytes 4640 | tf_op jit(solution)/shard_map/ppermute | solution.py:50
  (518 shorter events, 90.1 us)
Async XLA Ops:
  2.3 47.8 %collective-permute-start.1 = (f32[26,8,1,128]{3,2,1,0:T(1,128)}, f32[26,8,1,128]{3,2,1,0:T(1,128)S(1)}, u32[]{:S(2)}, u32[]{:S(2)}) collective-permute-start(f32[26,8,1,128]{3,2,1,0:T(1,128)} %get-tuple-element.168), channel_id=1, source_target_pairs={{8,0},{16,8},{24,16},{0,24},{9,1},{17,9},{25,17},{1,25},{10,2},{18... | collective-permute-start | bytes 319496 | tf_op jit(solution)/shard_map/ppermute | solution.py:51
  8.5 23.4 %collective-permute-start.25 = (f32[8,2,128]{2,1,0:T(2,128)S(1)}, f32[8,2,128]{2,1,0:T(2,128)S(1)}, u32[]{:S(2)}, u32[]{:S(2)}) collective-permute-start(f32[8,2,128]{2,1,0:T(2,128)S(1)} %get-tuple-element.236), channel_id=1, source_target_pairs={{8,0},{16,8},{24,16},{0,24},{9,1},{17,9},{25,17},{1,25},{10,2},{18... | collective-permute-start | bytes 24584 | tf_op jit(solution)/shard_map/ppermute | solution.py:51
  9.0 22.9 %collective-permute-start.24 = (f32[8,2,128]{2,1,0:T(2,128)S(1)}, f32[8,2,128]{2,1,0:T(2,128)S(1)}, u32[]{:S(2)}, u32[]{:S(2)}) collective-permute-start(f32[8,2,128]{2,1,0:T(2,128)S(1)} %get-tuple-element.235), channel_id=1, source_target_pairs={{0,8},{8,16},{16,24},{24,0},{1,9},{9,17},{17,25},{25,1},{2,10},{10... | collective-permute-start | bytes 24584 | tf_op jit(solution)/shard_map/ppermute | solution.py:50
  10.8 23.8 %collective-permute-start.7 = (f32[8,2,128]{2,1,0:T(2,128)S(1)}, f32[8,2,128]{2,1,0:T(2,128)S(1)}, u32[]{:S(2)}, u32[]{:S(2)}) collective-permute-start(f32[8,2,128]{2,1,0:T(2,128)S(1)} %get-tuple-element.246), channel_id=1, source_target_pairs={{8,0},{16,8},{24,16},{0,24},{9,1},{17,9},{25,17},{1,25},{10,2},{18... | collective-permute-start | bytes 24584 | tf_op jit(solution)/shard_map/ppermute | solution.py:51
  13.1 21.5 %collective-permute-start.6 = (f32[8,2,128]{2,1,0:T(2,128)S(1)}, f32[8,2,128]{2,1,0:T(2,128)S(1)}, u32[]{:S(2)}, u32[]{:S(2)}) collective-permute-start(f32[8,2,128]{2,1,0:T(2,128)S(1)} %get-tuple-element.245), channel_id=1, source_target_pairs={{0,8},{8,16},{16,24},{24,0},{1,9},{9,17},{17,25},{25,1},{2,10},{10... | collective-permute-start | bytes 24584 | tf_op jit(solution)/shard_map/ppermute | solution.py:50
  32.1 5.6 %collective-permute-start.27 = (f32[8,12,2]{2,1,0:T(8,128)S(1)}, f32[8,12,2]{2,1,0:T(8,128)S(1)}, u32[]{:S(2)}, u32[]{:S(2)}) collective-permute-start(f32[8,12,2]{2,1,0:T(8,128)S(1)} %get-tuple-element.224), channel_id=1, source_target_pairs={{2,0},{4,2},{6,4},{0,6},{3,1},{5,3},{7,5},{1,7},{10,8},{12,10},{14... | collective-permute-start | bytes 2312 | tf_op jit(solution)/shard_map/ppermute | solution.py:51
  34.6 5.8 %collective-permute-start.26 = (f32[8,12,2]{2,1,0:T(8,128)S(1)}, f32[8,12,2]{2,1,0:T(8,128)S(1)}, u32[]{:S(2)}, u32[]{:S(2)}) collective-permute-start(f32[8,12,2]{2,1,0:T(8,128)S(1)} %get-tuple-element.223), channel_id=1, source_target_pairs={{0,2},{2,4},{4,6},{6,0},{1,3},{3,5},{5,7},{7,1},{8,10},{10,12},{12... | collective-permute-start | bytes 2312 | tf_op jit(solution)/shard_map/ppermute | solution.py:50
  34.7 6.4 %collective-permute-start.9 = (f32[8,12,2]{2,1,0:T(8,128)S(1)}, f32[8,12,2]{2,1,0:T(8,128)S(1)}, u32[]{:S(2)}, u32[]{:S(2)}) collective-permute-start(f32[8,12,2]{2,1,0:T(8,128)S(1)} %get-tuple-element.226), channel_id=1, source_target_pairs={{2,0},{4,2},{6,4},{0,6},{3,1},{5,3},{7,5},{1,7},{10,8},{12,10},{14... | collective-permute-start | bytes 2312 | tf_op jit(solution)/shard_map/ppermute | solution.py:51
  37.6 5.2 %collective-permute-start.8 = (f32[8,12,2]{2,1,0:T(8,128)S(1)}, f32[8,12,2]{2,1,0:T(8,128)S(1)}, u32[]{:S(2)}, u32[]{:S(2)}) collective-permute-start(f32[8,12,2]{2,1,0:T(8,128)S(1)} %get-tuple-element.225), channel_id=1, source_target_pairs={{0,2},{2,4},{4,6},{6,0},{1,3},{3,5},{5,7},{7,1},{8,10},{10,12},{12... | collective-permute-start | bytes 2312 | tf_op jit(solution)/shard_map/ppermute | solution.py:50
  43.6 7.3 %collective-permute-start = (f32[26,8,1,128]{3,2,1,0:T(1,128)}, f32[26,8,1,128]{3,2,1,0:T(1,128)S(1)}, u32[]{:S(2)}, u32[]{:S(2)}) collective-permute-start(f32[26,8,1,128]{3,2,1,0:T(1,128)} %get-tuple-element.167), channel_id=1, source_target_pairs={{0,8},{8,16},{16,24},{24,0},{1,9},{9,17},{17,25},{25,1},{2,10},{10... | collective-permute-start | bytes 319496 | tf_op jit(solution)/shard_map/ppermute | solution.py:50
  56.6 5.0 %collective-permute-start.3 = (f32[26,8,10,1]{0,1,3,2:T(8,128)}, f32[26,8,10,1]{0,1,3,2:T(8,128)}, u32[]{:S(2)}, u32[]{:S(2)}) collective-permute-start(f32[26,8,10,1]{0,1,3,2:T(8,128)} %copy.117), channel_id=1, source_target_pairs={{2,0},{4,2},{6,4},{0,6},{3,1},{5,3},{7,5},{1,7},{10,8},{12,10},{14... | collective-permute-start | bytes 24968 | tf_op jit(solution)/shard_map/ppermute | solution.py:51
  58.1 5.9 %collective-permute-start.2 = (f32[26,8,10,1]{0,1,3,2:T(8,128)}, f32[26,8,10,1]{0,1,3,2:T(8,128)}, u32[]{:S(2)}, u32[]{:S(2)}) collective-permute-start(f32[26,8,10,1]{0,1,3,2:T(8,128)} %copy.116), channel_id=1, source_target_pairs={{0,2},{2,4},{4,6},{6,0},{1,3},{3,5},{5,7},{7,1},{8,10},{10,12},{12... | collective-permute-start | bytes 24968 | tf_op jit(solution)/shard_map/ppermute | solution.py:50
  86.7 5.5 %collective-permute-start.13 = (f32[6,8,2,128]{3,2,1,0:T(2,128)S(1)}, f32[6,8,2,128]{3,2,1,0:T(2,128)S(1)}, u32[]{:S(2)}, u32[]{:S(2)}) collective-permute-start(f32[6,8,2,128]{3,2,1,0:T(2,128)S(1)} %get-tuple-element.185), channel_id=1, source_target_pairs={{8,0},{16,8},{24,16},{0,24},{9,1},{17,9},{25,17},{1,25},{10,2},{18... | collective-permute-start | bytes 147464 | tf_op jit(solution)/shard_map/ppermute | solution.py:51
  90.4 5.9 %collective-permute-start.12 = (f32[6,8,2,128]{3,2,1,0:T(2,128)S(1)}, f32[6,8,2,128]{3,2,1,0:T(2,128)S(1)}, u32[]{:S(2)}, u32[]{:S(2)}) collective-permute-start(f32[6,8,2,128]{3,2,1,0:T(2,128)S(1)} %get-tuple-element.184), channel_id=1, source_target_pairs={{0,8},{8,16},{16,24},{24,0},{1,9},{9,17},{17,25},{25,1},{2,10},{10... | collective-permute-start | bytes 147464 | tf_op jit(solution)/shard_map/ppermute | solution.py:50
  96.5 12.1 %collective-permute-start.15 = (f32[6,8,12,2]{3,2,1,0:T(8,128)S(1)}, f32[6,8,12,2]{3,2,1,0:T(8,128)S(1)}, u32[]{:S(2)}, u32[]{:S(2)}) collective-permute-start(f32[6,8,12,2]{3,2,1,0:T(8,128)S(1)} %get-tuple-element.172), channel_id=1, source_target_pairs={{2,0},{4,2},{6,4},{0,6},{3,1},{5,3},{7,5},{1,7},{10,8},{12,10},{14... | collective-permute-start | bytes 13832 | tf_op jit(solution)/shard_map/ppermute | solution.py:51
  97.5 17.3 %collective-permute-start.14 = (f32[6,8,12,2]{3,2,1,0:T(8,128)S(1)}, f32[6,8,12,2]{3,2,1,0:T(8,128)S(1)}, u32[]{:S(2)}, u32[]{:S(2)}) collective-permute-start(f32[6,8,12,2]{3,2,1,0:T(8,128)S(1)} %get-tuple-element.171), channel_id=1, source_target_pairs={{0,2},{2,4},{4,6},{6,0},{1,3},{3,5},{5,7},{7,1},{8,10},{10,12},{12... | collective-permute-start | bytes 13832 | tf_op jit(solution)/shard_map/ppermute | solution.py:50
  118.8 7.4 %collective-permute-start.19 = (f32[26,8,1,128]{3,1,2,0:T(8,128)S(1)}, f32[26,8,1,128]{3,1,2,0:T(8,128)S(1)}, u32[]{:S(2)}, u32[]{:S(2)}) collective-permute-start(f32[26,8,1,128]{3,1,2,0:T(8,128)S(1)} %bitcast.479), channel_id=1, source_target_pairs={{8,0},{16,8},{24,16},{0,24},{9,1},{17,9},{25,17},{1,25},{10,2},{18... | collective-permute-start | bytes 319496 | tf_op jit(solution)/shard_map/ppermute | solution.py:51
  119.3 7.0 %collective-permute-start.18 = (f32[26,8,1,128]{3,1,2,0:T(8,128)S(1)}, f32[26,8,1,128]{3,1,2,0:T(8,128)S(1)}, u32[]{:S(2)}, u32[]{:S(2)}) collective-permute-start(f32[26,8,1,128]{3,1,2,0:T(8,128)S(1)} %bitcast.478), channel_id=1, source_target_pairs={{0,8},{8,16},{16,24},{24,0},{1,9},{9,17},{17,25},{25,1},{2,10},{10... | collective-permute-start | bytes 319496 | tf_op jit(solution)/shard_map/ppermute | solution.py:50
  131.2 4.3 %collective-permute-start.21 = (f32[26,8,10,1]{0,1,3,2:T(8,128)}, f32[26,8,10,1]{0,1,3,2:T(8,128)}, u32[]{:S(2)}, u32[]{:S(2)}) collective-permute-start(f32[26,8,10,1]{0,1,3,2:T(8,128)} %copy.125), channel_id=1, source_target_pairs={{2,0},{4,2},{6,4},{0,6},{3,1},{5,3},{7,5},{1,7},{10,8},{12,10},{14... | collective-permute-start | bytes 24968 | tf_op jit(solution)/shard_map/ppermute | solution.py:51
  134.3 5.2 %collective-permute-start.20 = (f32[26,8,10,1]{0,1,3,2:T(8,128)}, f32[26,8,10,1]{0,1,3,2:T(8,128)}, u32[]{:S(2)}, u32[]{:S(2)}) collective-permute-start(f32[26,8,10,1]{0,1,3,2:T(8,128)} %copy.124), channel_id=1, source_target_pairs={{0,2},{2,4},{4,6},{6,0},{1,3},{3,5},{5,7},{7,1},{8,10},{10,12},{12... | collective-permute-start | bytes 24968 | tf_op jit(solution)/shard_map/ppermute | solution.py:50
  156.3 4.1 %collective-permute-start.31 = (f32[6,8,2,128]{3,2,1,0:T(2,128)S(1)}, f32[6,8,2,128]{3,2,1,0:T(2,128)S(1)}, u32[]{:S(2)}, u32[]{:S(2)}) collective-permute-start(f32[6,8,2,128]{3,2,1,0:T(2,128)S(1)} %get-tuple-element.180), channel_id=1, source_target_pairs={{8,0},{16,8},{24,16},{0,24},{9,1},{17,9},{25,17},{1,25},{10,2},{18... | collective-permute-start | bytes 147464 | tf_op jit(solution)/shard_map/ppermute | solution.py:51
  156.9 5.9 %collective-permute-start.30 = (f32[6,8,2,128]{3,2,1,0:T(2,128)S(1)}, f32[6,8,2,128]{3,2,1,0:T(2,128)S(1)}, u32[]{:S(2)}, u32[]{:S(2)}) collective-permute-start(f32[6,8,2,128]{3,2,1,0:T(2,128)S(1)} %get-tuple-element.179), channel_id=1, source_target_pairs={{0,8},{8,16},{16,24},{24,0},{1,9},{9,17},{17,25},{25,1},{2,10},{10... | collective-permute-start | bytes 147464 | tf_op jit(solution)/shard_map/ppermute | solution.py:50
  163.1 12.1 %collective-permute-start.33 = (f32[6,8,12,2]{3,2,1,0:T(8,128)S(1)}, f32[6,8,12,2]{3,2,1,0:T(8,128)S(1)}, u32[]{:S(2)}, u32[]{:S(2)}) collective-permute-start(f32[6,8,12,2]{3,2,1,0:T(8,128)S(1)} %get-tuple-element.170), channel_id=1, source_target_pairs={{2,0},{4,2},{6,4},{0,6},{3,1},{5,3},{7,5},{1,7},{10,8},{12,10},{14... | collective-permute-start | bytes 13832 | tf_op jit(solution)/shard_map/ppermute | solution.py:51
  164.0 17.5 %collective-permute-start.32 = (f32[6,8,12,2]{3,2,1,0:T(8,128)S(1)}, f32[6,8,12,2]{3,2,1,0:T(8,128)S(1)}, u32[]{:S(2)}, u32[]{:S(2)}) collective-permute-start(f32[6,8,12,2]{3,2,1,0:T(8,128)S(1)} %get-tuple-element.169), channel_id=1, source_target_pairs={{0,2},{2,4},{4,6},{6,0},{1,3},{3,5},{5,7},{7,1},{8,10},{10,12},{12... | collective-permute-start | bytes 13832 | tf_op jit(solution)/shard_map/ppermute | solution.py:50
  (137 other events, 512.6 us)
where the time goes:
time: 187 us; the launch traced here: 186 us
  waiting for transfers between devices  59.1 us (32%)
  local copies, waits for them, and re-layouts  54.7 us (29%)
  other arithmetic  35.8 us (19%)
  starting transfers between devices  34.4 us (18%)
  between operations  2.3 us (1%)
    ppermute x18, waiting for transfers between devices, extended_2(): after = lax.ppermute(first, axis, down)  31.4 us
    ppermute x18, waiting for transfers between devices, extended_2(): before = lax.ppermute(last, axis, up)  27.7 us
    unnamed x331, local copies, waits for them, and re-layouts  23.5 us
    ppermute x18, starting transfers between devices, extended_2(): after = lax.ppermute(first, axis, down)  22 us
    ppermute x18, starting transfers between devices, extended_2(): before = lax.ppermute(last, axis, up)  12.4 us
    slice x11, local copies, waits for them, and re-layouts, extended_2(): last = lax.slice_in_dim(shard, length - width, length, axis=dim)  9.53 us
    concatenate x8, other arithmetic, extended_2(): shard = jnp.concatenate([before, shard, after], axis=dim)  7.87 us
    ppermute x2, local copies, waits for them, and re-layouts, extended_2(): before = lax.ppermute(last, axis, up)  6.78 us
  transfers between devices with their start and end apart: 36, of which 24 were waited for; matrix products, arithmetic and copies ran while one was open for 21% of the time, Pallas kernels for 0%

commit v1 on v0

v1 whole, which is shorter than its diff:
```python
import jax
import jax.numpy as jnp
import numpy as np
from jax import lax
from jax.experimental import pallas as pl
from jax.experimental.pallas import tpu as pltpu
from jax.sharding import PartitionSpec as P

VELOCITY = [
    (0, 0, 0),
    (1, 0, 0),
    (-1, 0, 0),
    (0, 1, 0),
    (0, -1, 0),
    (0, 0, 1),
    (0, 0, -1),
    (1, 1, 0),
    (-1, -1, 0),
    (1, -1, 0),
    (-1, 1, 0),
    (1, 0, 1),
    (-1, 0, -1),
    (1, 0, -1),
    (-1, 0, 1),
    (0, 1, 1),
    (0, -1, -1),
    (0, 1, -1),
    (0, -1, 1),
]
OPPOSITE = [0, 2, 1, 4, 3, 6, 5, 8, 7, 10, 9, 12, 11, 14, 13, 16, 15, 18, 17]
VELOCITY = VELOCITY + VELOCITY[:7]
OPPOSITE = OPPOSITE + [19 + mirror for mirror in OPPOSITE[:7]]
WELL = 1.2
STIFFNESS = 0.6
SHARPEN = 0.3
PHASE_RATE = 1.4
MESH = pl.DeviceIdType.MESH

RISING = [i for i in range(26) if VELOCITY[i][0] == 1]
FALLING = [i for i in range(26) if VELOCITY[i][0] == -1]
ALONG_X = {sign: [i for i in range(26) if VELOCITY[i][1] == sign] for sign in (1, -1)}
ALONG_Y = {sign: [i for i in range(26) if VELOCITY[i][2] == sign] for sign in (1, -1)}
DIAGONAL = {VELOCITY[i][1:]: i for i in range(15, 19)}
SIDES = [(-1, 0), (1, 0), (0, -1), (0, 1)]
CORNERS = [(-1, -1), (-1, 1), (1, -1), (1, 1)]
SLOT = {way: i for i, way in enumerate(SIDES)}
SLOT.update({way: i for i, way in enumerate(CORNERS)})


def kernel(
    pop0, pop1, cot, out,
    adj_a, adj_b, phase, grads, sens, phibar, slope, phi,
    z1s, z1r, face1s, face1r, diag1s, diag1r, face0r, diag0s, diag0r,
    z2s, z2r, zd2s, zd2r, face2s, face2r, diag2s, diag2r, d2s, d2r, e2s, e2r,
    z3s, z3r, y3r, x3s, x3r,
    zd4s, zd4r, d4s, d4r, e4s, e4r,
    send_sem, recv_sem,
):
    gx, gy, gz = lax.axis_index("gx"), lax.axis_index("gy"), lax.axis_index("gz")
    nx, ny = lax.axis_size("gx"), lax.axis_size("gy")
    low = gz == 0
    partner = (gx, gy, 1 - gz)

    def device(way):
        return (lax.rem(gx + way[0] + nx, nx), lax.rem(gy + way[1] + ny, ny), gz)

    barrier = pltpu.get_barrier_semaphore()
    for target in [partner] + [device(way) for way in SIDES + CORNERS]:
        pl.semaphore_signal(barrier, inc=1, device_id=target, device_id_type=MESH)

    copies = []

    def send(src, dst, target):
        index = len(copies)
        copy = pltpu.make_async_remote_copy(
            src_ref=src,
            dst_ref=dst,
            send_sem=send_sem.at[index],
            recv_sem=recv_sem.at[index],
            device_id=target,
            device_id_type=MESH,
        )
        copy.start()
        copies.append(copy)
        return copy

    def arrive(group):
        for copy in group:
            copy.wait_recv()

    row = lax.broadcasted_iota(jnp.int32, (8, 128), 0)
    lane = lax.broadcasted_iota(jnp.int32, (8, 128), 1)
    row3 = lax.broadcasted_iota(jnp.int32, (8, 8, 128), 1)
    lane3 = lax.broadcasted_iota(jnp.int32, (8, 8, 128), 2)

    def zeros(*shape):
        return jnp.zeros(shape, jnp.float32)

    def roll(values, shift, axis):
        shift = shift % values.shape[axis]
        return values if shift == 0 else pltpu.roll(values, shift, axis)

    def layers(values, before, after):
        shape = values.shape[1:]
        parts = [zeros(before, *shape)] if before else []
        parts.append(values)
        if after:
            parts.append(zeros(after, *shape))
        return jnp.concatenate(parts, 0)

    def torus(center, rows, lanes, both):
        return jnp.concatenate(
            [jnp.concatenate([center, lanes], 2), jnp.concatenate([rows, both], 2)], 1
        )

    def embed(center):
        nothing = jnp.zeros_like(center)
        return torus(center, nothing, nothing, nothing)

    def vertical_layers(adj):
        return [jnp.where(low, adj[FALLING[k], 8], adj[RISING[k], 1]) for k in range(6)]

    def take_vertical(adj, ref, start):
        for k in range(6):
            layer = ref[start + k]
            adj[RISING[k], 9] = layer
            adj[FALLING[k], 0] = layer

    def pack_x(adj, sign):
        source = 0 if sign == 1 else 7
        packed = None
        for k, i in enumerate(ALONG_X[sign]):
            values = roll(adj[i, 1 + VELOCITY[i][0] : 9 + VELOCITY[i][0]], k - source, 1)
            packed = values if packed is None else jnp.where(row3 == k, values, packed)
        return packed

    def pack_y(adj, sign):
        source = 0 if sign == 1 else 127
        packed = None
        for k, i in enumerate(ALONG_Y[sign]):
            values = roll(adj[i, 1 + VELOCITY[i][0] : 9 + VELOCITY[i][0]], k - source, 2)
            packed = values if packed is None else jnp.where(lane3 == k, values, packed)
        return packed

    def edge_row(sign):
        return 0 if sign == 1 else 7

    def phase_gradients(which, face, diag, start):
        center = phase[which]
        prev_x, next_x = face[SLOT[(1, 0)], :10], face[SLOT[(-1, 0)], :10]
        prev_y, next_y = face[SLOT[(0, 1)], :10], face[SLOT[(0, -1)], :10]
        row10 = lax.broadcasted_iota(jnp.int32, (10, 8, 128), 1)
        lane10 = lax.broadcasted_iota(jnp.int32, (10, 8, 128), 2)
        rows = layers(jnp.where(row10 < 4, next_x, prev_x), 1, 1)
        lanes = layers(jnp.where(lane10 < 64, next_y, prev_y), 1, 1)

        def corner(way):
            return diag[SLOT[way], start]

        lane_z = lax.broadcasted_iota(jnp.int32, (8, 128), 1)
        ahead = jnp.where(lane_z < 64, corner((-1, -1)), corner((-1, 1)))
        behind = jnp.where(lane_z < 64, corner((1, -1)), corner((1, 1)))
        both = jnp.where(
            row3 < 4,
            jnp.broadcast_to(ahead[:, None, :], (8, 8, 128)),
            jnp.broadcast_to(behind[:, None, :], (8, 8, 128)),
        )
        ext = torus(center, rows, lanes, layers(both, 2, 2))
        slope[which] = WELL * (3.0 * ext * ext - 3.0 * ext + 0.5)
        mid = ext[1:11]
        x_up, x_down = roll(mid, -1, 1), roll(mid, 1, 1)
        y_up, y_down = roll(mid, -1, 2), roll(mid, 1, 2)
        lap = ext[:10] + ext[2:] + x_up + x_down + y_up + y_down - 6.0 * mid
        pot = WELL * mid * (mid - 1.0) * (mid - 0.5) - STIFFNESS * lap
        pot = jnp.concatenate(
            [jnp.where(low, 0.0, pot[:1]), pot[1:9], jnp.where(low, pot[9:], 0.0)], 0
        )
        grads[which, 0] = 0.5 * (center[3:11] - center[1:9])
        grads[which, 1] = 0.5 * (x_up - x_down)[1:9, :8, :128]
        grads[which, 2] = 0.5 * (y_up - y_down)[1:9, :8, :128]
        grads[which, 3] = 0.5 * (pot[2:, :8, :128] - pot[:8, :8, :128])
        inner = pot[1:9]
        grads[which, 4] = 0.5 * (roll(inner, -1, 1) - roll(inner, 1, 1))[:, :8, :128]
        grads[which, 5] = 0.5 * (roll(inner, -1, 2) - roll(inner, 1, 2))[:, :8, :128]

    def collide_adjoint(which, pop, adj, face, start, diag, tile, result, shift, with_phi):
        def layer(z, carry):
            def bounce(i, own, bounced):
                if VELOCITY[i][0] == 1:
                    return jnp.where(jnp.logical_and(z == 7, jnp.logical_not(low)), bounced, own)
                if VELOCITY[i][0] == -1:
                    return jnp.where(jnp.logical_and(z == 0, low), bounced, own)
                return own

            def arrived(i):
                cz, cx, cy = VELOCITY[i]
                own = adj[i, z + (1 + cz)]
                erow = 7 if cx == 1 else 0
                elane = 127 if cy == 1 else 0
                moved = own
                if cx:
                    k = ALONG_X[cx].index(i)
                    got = roll(face[SLOT[(-cx, 0)], start + z], erow - k, 0)
                    moved = jnp.where(row == erow, got, roll(own, -cx, 0))
                if cy:
                    k = ALONG_Y[cy].index(i)
                    got = roll(face[SLOT[(0, -cy)], start + z], elane - k, 1)
                    if cx:
                        corner = diag[SLOT[(-cx, -cy)], tile, pl.ds(z, 1), :]
                        corner = roll(jnp.broadcast_to(corner, (8, 128)), -cy, 1)
                        got = jnp.where(row == erow, corner, roll(got, -cx, 0))
                    moved = jnp.where(lane == elane, got, roll(moved, -cy, 1))
                return bounce(i, moved, adj[OPPOSITE[i], z + 1])

            def arrived_phi(i):
                cz, cx, cy = VELOCITY[i]
                own = phi[z + (1 + cz)]
                if cx:
                    erow = 7 if cx == 1 else 0
                    got = jnp.broadcast_to(x3r[SLOT[(-cx, 0)], pl.ds(z, 1), :], (8, 128))
                    own = jnp.where(row == erow, got, roll(own, -cx, 0))
                if cy:
                    elane = 127 if cy == 1 else 0
                    got = roll(y3r[SLOT[(0, -cy)] - 2, z], -cy, 1)
                    own = jnp.where(lane == elane, got, roll(own, -cy, 1))
                return bounce(i, own, phi[z + 1])

            a = [arrived(i) for i in range(26)]
            if with_phi:
                a = a[:19] + [a[i] + arrived_phi(i) for i in range(19, 26)]
            f = [pop[i, z].astype(jnp.float32) for i in range(19)]

            def total(values):
                values = list(values)
                while len(values) > 1:
                    values = [
                        values[j] + values[j + 1] if j + 1 < len(values) else values[j]
                        for j in range(0, len(values), 2)
                    ]
                return values[0]

            def signed(values, weight):
                plus = [values[i] for i in range(len(values)) if weight(i) == 1]
                minus = [values[i] for i in range(len(values)) if weight(i) == -1]
                return total(plus) - total(minus)

            def part(d):
                return lambda i: VELOCITY[i][d]

            def pair(d, e):
                return lambda i: VELOCITY[i][d] * VELOCITY[i][e]

            frac = phase[which, z + 2]
            pressure = total(f)
            momentum = [signed(f, part(d)) for d in range(3)]
            wa = [a[0] * (1.0 / 3.0)]
            wa += [a[i] * (1.0 / 18.0) for i in range(1, 7)]
            wa += [a[i] * (1.0 / 36.0) for i in range(7, 19)]
            a0 = total(wa)
            a1 = [signed(wa, part(d)) for d in range(3)]
            a2 = {}
            for d in range(3):
                a2[d, d] = total([wa[i] for i in range(19) if VELOCITY[i][d]])
                for e in range(d):
                    a2[d, e] = a2[e, d] = signed(wa, pair(d, e))
            af = total([a[i] * f[i] for i in range(19)])
            g = a[19:]
            b0 = 0.25 * g[0] + 0.125 * total(g[1:])
            b1 = [0.125 * (g[1 + 2 * d] - g[2 + 2 * d]) for d in range(3)]

            def dot(u, v):
                return u[0] * v[0] + u[1] * v[1] + u[2] * v[2]

            density = 0.2 + 0.8 * frac
            rate = 1.1 + 0.5 * frac
            half = 1.0 - 0.5 * rate
            pg = [grads[which, d, z] for d in range(3)]
            mg = [grads[which, 3 + d, z] for d in range(3)]
            force = [-frac * m for m in mg]
            inverse = 1.0 / density
            u = [(momentum[d] + 0.5 * force[d]) * inverse for d in range(3)]
            a2u = [dot([a2[d, e] for e in range(3)], u) for d in range(3)]
            a2f = [dot([a2[d, e] for e in range(3)], force) for d in range(3)]
            speed = dot(u, u)
            quad = 3.0 * dot(u, a1) + 4.5 * dot(u, a2u) - 1.5 * speed * a0
            slant = [3.0 * a1[d] - 3.0 * a0 * u[d] + 9.0 * a2u[d] for d in range(3)]
            rate_density = rate * density
            phase_pull = (4.0 * PHASE_RATE) * frac
            ubar = [
                rate_density * slant[d]
                + half * (9.0 * a2f[d] - 3.0 * a0 * force[d])
                + phase_pull * b1[d]
                for d in range(3)
            ]
            jbar = [ubar[d] * inverse for d in range(3)]
            fbar = [half * slant[d] + 0.5 * jbar[d] for d in range(3)]
            density_bar = rate * quad - dot(jbar, u)
            rate_bar = pressure * a0 + density * quad - af - 0.5 * dot(force, slant)
            imag = lax.rsqrt(dot(pg, pg) + 0.0625)
            normal = [p * imag for p in pg]
            nb1 = dot(normal, b1)
            frac_bar = (
                0.5 * rate_bar
                + 0.8 * density_bar
                - dot(mg, fbar)
                + PHASE_RATE * (b0 + 4.0 * dot(u, b1))
                + (PHASE_RATE * 4.0 * SHARPEN) * (1.0 - 2.0 * frac) * nb1
            )
            pull = (PHASE_RATE * 4.0 * SHARPEN) * frac * (1.0 - frac) * imag
            for d in range(3):
                sens[d, z] = pull * (b1[d] - normal[d] * nb1)
                sens[3 + d, z] = -frac * fbar[d]
            phibar[z] = frac_bar
            pbar = rate * a0
            keep = 1.0 - rate
            for i in range(19):
                value = keep * a[i] + pbar
                for d in range(3):
                    if VELOCITY[i][d] == 1:
                        value = value + jbar[d]
                    elif VELOCITY[i][d] == -1:
                        value = value - jbar[d]
                result[i, z + shift] = value
            for k in range(7):
                result[19 + k, z + shift] = (1.0 - PHASE_RATE) * g[k]
            return carry

        lax.fori_loop(0, 8, layer, 0)

    def phase_share(which):
        def spread(first):
            vz = embed(sens[first])
            vx = embed(sens[first + 1])
            vy = embed(sens[first + 2])
            flat = roll(vx, 1, 1) - roll(vx, -1, 1) + roll(vy, 1, 2) - roll(vy, -1, 2)
            return 0.5 * (layers(flat, 1, 1) + layers(vz, 2, 0) - layers(vz, 0, 2))

        mu = spread(3)
        mu = jnp.concatenate(
            [jnp.where(low, 0.0, mu[:1]), mu[1:9], jnp.where(low, mu[9:], 0.0)], 0
        )
        flat = roll(mu, 1, 1) + roll(mu, -1, 1) + roll(mu, 1, 2) + roll(mu, -1, 2) - 6.0 * mu
        lap = layers(flat, 1, 1) + layers(mu, 2, 0) + layers(mu, 0, 2)
        rest = spread(0) + layers(embed(phibar[...]), 1, 1)
        return slope[which] * layers(mu, 1, 1) - STIFFNESS * lap + layers(rest, 1, 1)

    def send_share(share, zs, zr):
        edge = jnp.where(low, share[10:], share[:2])
        zs[...] = edge
        return send(zs, zr, partner)

    def share_sides(share, zcopy, zr, ds, dr, es, er):
        zcopy.wait_recv()
        extra = zr[...]
        lower = share[2:4] + jnp.where(low, 0.0, extra)
        upper = share[8:10] + jnp.where(low, extra, 0.0)
        share = jnp.concatenate([lower, share[4:8], upper], 0)
        ds[0] = share[:, 8:, :128]
        ds[1] = share[:, :8, 128:]
        es[0] = share[:, 15, 128:]
        es[1] = share[:, 8, 128:]
        group = []
        for way in SIDES:
            source = ds.at[0] if way[0] else ds.at[1]
            group.append(send(source, dr.at[SLOT[way]], device(way)))
        for way in CORNERS:
            group.append(send(es.at[0 if way[0] < 0 else 1], er.at[SLOT[way]], device(way)))
        return share[:, :8, :128], group

    def collect_share(center, group, dr, er):
        arrive(group)
        total = center
        total = total + jnp.where(row3 < 2, dr[SLOT[(1, 0)]], 0.0)
        total = total + jnp.where(row3 >= 6, dr[SLOT[(-1, 0)]], 0.0)
        total = total + jnp.where(lane3 < 2, dr[SLOT[(0, 1)]], 0.0)
        total = total + jnp.where(lane3 >= 126, dr[SLOT[(0, -1)]], 0.0)
        for way in CORNERS:
            at_row = row3 == (0 if way[0] == 1 else 7)
            at_lane = lane3 == (0 if way[1] == 1 else 127)
            wide = jnp.broadcast_to(er[SLOT[way]][:, None, :], (8, 8, 128))
            total = total + jnp.where(jnp.logical_and(at_row, at_lane), wide, 0.0)
        return total

    for which, pop in ((0, pop0), (1, pop1)):
        terms = [pop[i].astype(jnp.float32) for i in range(19, 26)]
        value = terms[0]
        for term in terms[1:]:
            value = value + term
        phase[which, 2:10] = value
    for which in range(2):
        z1s[2 * which : 2 * which + 2] = jnp.where(low, phase[which, 8:10], phase[which, 2:4])
    for k in range(6):
        z1s[4 + k] = jnp.where(low, cot[FALLING[k], 7], cot[RISING[k], 0])
    pl.semaphore_wait(barrier, 9)
    vertical = send(z1s, z1r, partner)
    for i in range(26):
        adj_a[i, 1:9] = cot[i]
    vertical.wait_recv()
    for which in range(2):
        got = z1r[2 * which : 2 * which + 2]
        phase[which, :2] = jnp.where(low, 0.0, got)
        phase[which, 10:] = jnp.where(low, got, 0.0)
    take_vertical(adj_a, z1r, 4)

    first = []
    for way in CORNERS:
        slot = SLOT[way]
        i = DIAGONAL[(-way[0], -way[1])]
        r = edge_row(-way[0])
        diag1s[slot, 0] = phase[1, 2:10, r, :]
        diag1s[slot, 1] = phase[0, 2:10, r, :]
        diag1s[slot, 2] = adj_a[i, 1:9, r, :]
        first.append(send(diag1s.at[slot], diag1r.at[slot], device(way)))
    for way in SIDES:
        slot = SLOT[way]
        face1s[slot, :10] = phase[1, 1:11]
        face1s[slot, 10:] = pack_x(adj_a, -way[0]) if way[0] else pack_y(adj_a, -way[1])
        first.append(send(face1s.at[slot], face1r.at[slot], device(way)))
    later = []
    for way in SIDES:
        slot = SLOT[way]
        later.append(send(phase.at[0, pl.ds(1, 10)], face0r.at[slot], device(way)))
    arrive(first)
    phase_gradients(1, face1r, diag1r, 0)
    collide_adjoint(1, pop1, adj_a, face1r, 10, diag1r, 2, adj_b, 1, False)

    for k, layer in enumerate(vertical_layers(adj_b)):
        z2s[k] = layer
    vertical = send(z2s, z2r, partner)
    share = phase_share(1)
    zcopy = send_share(share, zd2s, zd2r)
    vertical.wait_recv()
    take_vertical(adj_b, z2r, 0)
    second = []
    for way in CORNERS:
        slot = SLOT[way]
        diag2s[slot, 0] = adj_b[DIAGONAL[(-way[0], -way[1])], 1:9, edge_row(-way[0]), :]
        second.append(send(diag2s.at[slot], diag2r.at[slot], device(way)))
    for way in SIDES:
        slot = SLOT[way]
        face2s[slot] = pack_x(adj_b, -way[0]) if way[0] else pack_y(adj_b, -way[1])
        second.append(send(face2s.at[slot], face2r.at[slot], device(way)))
    center, group = share_sides(share, zcopy, zd2r, d2s, d2r, e2s, e2r)
    arrive(later)
    phase_gradients(0, face0r, diag1r, 1)
    phi[1:9] = collect_share(center, group, d2r, e2r)
    z3s[...] = jnp.where(low, phi[8], phi[1])
    third = [send(z3s, z3r, partner)]
    for way in SIDES:
        slot = SLOT[way]
        if way[0]:
            x3s[slot] = phi[1:9, edge_row(-way[0]), :]
            third.append(send(x3s.at[slot], x3r.at[slot], device(way)))
        else:
            third.append(send(phi.at[pl.ds(1, 8)], y3r.at[slot - 2], device(way)))
    arrive(second)
    arrive(third)
    phi[0] = z3r[...]
    phi[9] = z3r[...]
    collide_adjoint(0, pop0, adj_b, face2r, 0, diag2r, 0, out, 0, True)

    share = phase_share(0)
    zcopy = send_share(share, zd4s, zd4r)
    center, group = share_sides(share, zcopy, zd4r, d4s, d4r, e4s, e4r)
    total = collect_share(center, group, d4r, e4r)
    for k in range(7):
        out[19 + k] = out[19 + k] + total
    for copy in copies:
        copy.wait_send()


def local(populations0, populations1, cotangent):
    def vmem(*shape):
        return pltpu.VMEM(shape, jnp.float32)

    tile = (8, 128)
    scratch = [
        vmem(26, 10, *tile),
        vmem(26, 10, *tile),
        vmem(2, 12, *tile),
        vmem(2, 6, 8, *tile),
        vmem(6, 8, *tile),
        vmem(8, *tile),
        vmem(2, 12, 16, 256),
        vmem(10, *tile),
        vmem(10, *tile),
        vmem(10, *tile),
        vmem(4, 18, *tile),
        vmem(4, 18, *tile),
        vmem(4, 3, *tile),
        vmem(4, 3, *tile),
        vmem(4, 10, *tile),
        vmem(1, *tile),
        vmem(1, *tile),
        vmem(6, *tile),
        vmem(6, *tile),
        vmem(2, 16, 256),
        vmem(2, 16, 256),
        vmem(4, 8, *tile),
        vmem(4, 8, *tile),
        vmem(4, 1, *tile),
        vmem(4, 1, *tile),
        vmem(2, 8, *tile),
        vmem(4, 8, *tile),
        vmem(2, *tile),
        vmem(4, *tile),
        vmem(*tile),
        vmem(*tile),
        vmem(2, 8, *tile),
        vmem(2, *tile),
        vmem(2, *tile),
        vmem(2, 16, 256),
        vmem(2, 16, 256),
        vmem(2, 8, *tile),
        vmem(4, 8, *tile),
        vmem(2, *tile),
        vmem(4, *tile),
        pltpu.SemaphoreType.DMA((48,)),
        pltpu.SemaphoreType.DMA((48,)),
    ]
    return pl.pallas_call(
        kernel,
        out_shape=jax.ShapeDtypeStruct(cotangent.shape, jnp.float32),
        in_specs=[pl.BlockSpec(memory_space=pltpu.VMEM)] * 3,
        out_specs=pl.BlockSpec(memory_space=pltpu.VMEM),
        scratch_shapes=scratch,
        compiler_params=pltpu.CompilerParams(
            collective_id=0, has_side_effects=True, vmem_limit_bytes=40 * 1024 * 1024
        ),
    )(populations0, populations1, cotangent)


def solution(mesh):
    spec = P(None, "gz", "gx", "gy")
    return jax.shard_map(
        local, mesh=mesh, in_specs=(spec, spec, spec), out_specs=spec, check_vma=False
    )
```

time: 187 us -> 38.6 us (0.21)
  waiting for transfers between devices: 59.1 us -> 0 us
  local copies, waits for them, and re-layouts: 54.7 us -> 4.07 us
  other arithmetic: 35.8 us -> 0 us
  starting transfers between devices: 34.4 us -> 0 us
  Pallas kernels: 0 us -> 34.3 us
  between operations: 2.3 us -> 0.01 us
    ppermute x36 -> x0, waiting for transfers between devices: 59.1 us -> none  [the longest x18 31.4 us: extended_2(): after = lax.ppermute(first, axis, down)]
    ppermute x36 -> x0, starting transfers between devices: 34.4 us -> none  [the longest x18 22 us: extended_2(): after = lax.ppermute(first, axis, down)]
    pallas_call x0 -> x1, Pallas kernels: none -> 34.3 us  [local(): pl.pallas_call(kernel, out_shape=jax.ShapeDtypeStruct(cotangent.shape, jn...]
    unnamed x331 -> x7, local copies, waits for them, and re-layouts: 23.5 us -> 4.07 us
    slice x13 -> x0, local copies, waits for them, and re-layouts: 15.2 us -> none  [the longest x11 9.53 us: extended_2(): last = lax.slice_in_dim(shard, length - width, length, axis=dim)]
    ppermute x4 -> x0, local copies, waits for them, and re-layouts: 11.5 us -> none  [the longest x2 6.78 us: extended_2(): before = lax.ppermute(last, axis, up)]
    concatenate x9 -> x0, other arithmetic: 8.86 us -> none  [the longest x8 7.87 us: extended_2(): shard = jnp.concatenate([before, shard, after], axis=dim)]
    reduce_sum x17 -> x0, other arithmetic: 6.5 us -> none  [the longest x2 2.51 us: collide(): relax_rate * (flow_part - flow_equil)]
  transfers between devices with their start and end apart: 36 -> 0, of which waited for: 24 -> 0; matrix products, arithmetic and copies ran while one was open for 21% -> 0% of each run, Pallas kernels for 0% -> 0%
where the time goes in v1:
time: 38.6 us; the launch traced here: 38.3 us
  Pallas kernels  34.3 us (89%)
  local copies, waits for them, and re-layouts  4.07 us (11%)
    pallas_call x1, Pallas kernels, local(): pl.pallas_call(kernel, out_shape=jax.ShapeDtypeStruct(cotangent.shape, jn...  34.3 us
    unnamed x7, local copies, waits for them, and re-layouts  4.07 us

profile of v1, /device:TPU:0, one launch (start us, length us, event | category | flops | bytes accessed | tf_op | source)
XLA Modules:
  0.0 38.3 jit_solution(16116548961677670887)
XLA Ops:
  0.0 0.0 copy-start
  0.0 1.2 %copy-done = f32[26,8,8,128]{3,2,1,0:T(8,128)S(1)} copy-done((f32[26,8,8,128]{3,2,1,0:T(8,128)S(1)}, f32[26,8,8,128]{3,2,1,0:T(8,128)}, u32[]{:S(2)}) %copy-start) | copy-done | bytes 851992
  1.2 0.0 copy-start.1
  1.2 1.0 %copy-done.1 = bf16[26,8,8,128]{3,2,1,0:T(8,128)(2,1)S(1)} copy-done((bf16[26,8,8,128]{3,2,1,0:T(8,128)(2,1)S(1)}, bf16[26,8,8,128]{3,2,1,0:T(8,128)(2,1)}, u32[]{:S(2)}) %copy-start.1) | copy-done | bytes 426008
  2.2 0.0 copy-start.2
  2.2 1.0 %copy-done.2 = bf16[26,8,8,128]{3,2,1,0:T(8,128)(2,1)S(1)} copy-done((bf16[26,8,8,128]{3,2,1,0:T(8,128)(2,1)S(1)}, bf16[26,8,8,128]{3,2,1,0:T(8,128)(2,1)}, u32[]{:S(2)}) %copy-start.2) | copy-done | bytes 426008
  3.2 34.3 %shard_map.37 = f32[26,8,8,128]{3,2,1,0:T(8,128)S(1)} custom-call(bf16[26,8,8,128]{3,2,1,0:T(8,128)(2,1)S(1)} %copy-done.1, bf16[26,8,8,128]{3,2,1,0:T(8,128)(2,1)S(1)} %copy-done.2, f32[26,8,8,128]{3,2,1,0:T(8,128)S(1)} %copy-done), custom_call_target="tpu_custom_call" | custom-call | tf_op jit(solution)/shard_map/pallas_call | solution.py:521
  37.4 0.9 %copy.5 = f32[26,8,8,128]{3,2,1,0:T(8,128)} copy(f32[26,8,8,128]{3,2,1,0:T(8,128)S(1)} %shard_map.37) | data formatting | bytes 1703936
Async XLA Ops:
  0.0 1.2 %copy-start = (f32[26,8,8,128]{3,2,1,0:T(8,128)S(1)}, f32[26,8,8,128]{3,2,1,0:T(8,128)}, u32[]{:S(2)}) copy-start(f32[26,8,8,128]{3,2,1,0:T(8,128)} %cot.1) | copy-start | bytes 2555908
  1.2 1.0 %copy-start.1 = (bf16[26,8,8,128]{3,2,1,0:T(8,128)(2,1)S(1)}, bf16[26,8,8,128]{3,2,1,0:T(8,128)(2,1)}, u32[]{:S(2)}) copy-start(bf16[26,8,8,128]{3,2,1,0:T(8,128)(2,1)} %pop0.1) | copy-start | bytes 1277956
  2.2 1.0 %copy-start.2 = (bf16[26,8,8,128]{3,2,1,0:T(8,128)(2,1)S(1)}, bf16[26,8,8,128]{3,2,1,0:T(8,128)(2,1)}, u32[]{:S(2)}) copy-start(bf16[26,8,8,128]{3,2,1,0:T(8,128)(2,1)} %pop1.1) | copy-start | bytes 1277956

commit v2 on v1

v2 whole, which is shorter than its diff:
```python
import jax
import jax.numpy as jnp
import numpy as np
from jax import lax
from jax.experimental import pallas as pl
from jax.experimental.pallas import tpu as pltpu
from jax.sharding import PartitionSpec as P

VELOCITY = [
    (0, 0, 0),
    (1, 0, 0),
    (-1, 0, 0),
    (0, 1, 0),
    (0, -1, 0),
    (0, 0, 1),
    (0, 0, -1),
    (1, 1, 0),
    (-1, -1, 0),
    (1, -1, 0),
    (-1, 1, 0),
    (1, 0, 1),
    (-1, 0, -1),
    (1, 0, -1),
    (-1, 0, 1),
    (0, 1, 1),
    (0, -1, -1),
    (0, 1, -1),
    (0, -1, 1),
]
OPPOSITE = [0, 2, 1, 4, 3, 6, 5, 8, 7, 10, 9, 12, 11, 14, 13, 16, 15, 18, 17]
VELOCITY = VELOCITY + VELOCITY[:7]
OPPOSITE = OPPOSITE + [19 + mirror for mirror in OPPOSITE[:7]]
WELL = 1.2
STIFFNESS = 0.6
SHARPEN = 0.3
PHASE_RATE = 1.4
MESH = pl.DeviceIdType.MESH

RISING = [i for i in range(26) if VELOCITY[i][0] == 1]
FALLING = [i for i in range(26) if VELOCITY[i][0] == -1]
ALONG_X = {sign: [i for i in range(26) if VELOCITY[i][1] == sign] for sign in (1, -1)}
ALONG_Y = {sign: [i for i in range(26) if VELOCITY[i][2] == sign] for sign in (1, -1)}
DIAGONAL = {VELOCITY[i][1:]: i for i in range(15, 19)}
SIDES = [(-1, 0), (1, 0), (0, -1), (0, 1)]
CORNERS = [(-1, -1), (-1, 1), (1, -1), (1, 1)]
SLOT = {way: i for i, way in enumerate(SIDES)}
SLOT.update({way: i for i, way in enumerate(CORNERS)})


def kernel(
    pop0_hbm, pop1_hbm, cot_hbm, out,
    pop0, pop1, adj_a, adj_b, phase, grads, sens, phibar, slope, phi, flow, moments, arrive_f,
    z1s, z1r, x1s, x1r, y1s, y1r, c1s, c1r,
    z2s, z2r, x2s, x2r, y2s, y2r, c2s, c2r,
    zd2s, zd2r, xd2s, xd2r, yd2s, yd2r, cd2s, cd2r,
    z3s, z3r, x3s, x3r, y3r,
    zd4s, zd4r, xd4s, xd4r, yd4s, yd4r, cd4s, cd4r,
    send_sem, recv_sem, load_sem,
):
    gx, gy, gz = lax.axis_index("gx"), lax.axis_index("gy"), lax.axis_index("gz")
    nx, ny = lax.axis_size("gx"), lax.axis_size("gy")
    low = gz == 0
    partner = (gx, gy, 1 - gz)
    pops = (pop0, pop1)

    def load(src, dst, index):
        copy = pltpu.make_async_copy(src, dst, load_sem.at[index])
        copy.start()
        return copy

    load_phase = [
        load(pop1_hbm.at[pl.ds(19, 7)], pop1.at[pl.ds(19, 7)], 0),
        load(pop0_hbm.at[pl.ds(19, 7)], pop0.at[pl.ds(19, 7)], 1),
    ]
    load_cot = [
        load(cot_hbm.at[pl.ds(0, 13)], adj_a.at[pl.ds(0, 13), pl.ds(1, 8)], 2),
        load(cot_hbm.at[pl.ds(13, 13)], adj_a.at[pl.ds(13, 13), pl.ds(1, 8)], 3),
    ]
    load_flow = [
        load(pop0_hbm.at[pl.ds(0, 19)], pop0.at[pl.ds(0, 19)], 4),
        load(pop1_hbm.at[pl.ds(0, 19)], pop1.at[pl.ds(0, 19)], 5),
    ]

    def device(way):
        return (lax.rem(gx + way[0] + nx, nx), lax.rem(gy + way[1] + ny, ny), gz)

    barrier = pltpu.get_barrier_semaphore()
    for target in [partner] + [device(way) for way in SIDES + CORNERS]:
        pl.semaphore_signal(barrier, inc=1, device_id=target, device_id_type=MESH)

    copies = []

    def send(src, dst, target):
        index = len(copies)
        copy = pltpu.make_async_remote_copy(
            src_ref=src,
            dst_ref=dst,
            send_sem=send_sem.at[index],
            recv_sem=recv_sem.at[index],
            device_id=target,
            device_id_type=MESH,
        )
        copy.start()
        copies.append(copy)
        return copy

    def arrive(group):
        for copy in group:
            copy.wait_recv()

    row = lax.broadcasted_iota(jnp.int32, (8, 128), 0)
    lane = lax.broadcasted_iota(jnp.int32, (8, 128), 1)

    def rows_of(count):
        return lax.broadcasted_iota(jnp.int32, (count, 8, 128), 1)

    def lanes_of(count):
        return lax.broadcasted_iota(jnp.int32, (count, 8, 128), 2)

    row3, lane3 = rows_of(8), lanes_of(8)

    def roll(values, shift, axis):
        shift = shift % values.shape[axis]
        return values if shift == 0 else pltpu.roll(values, shift, axis)

    def layers(values, before, after):
        shape = values.shape[1:]
        parts = [jnp.zeros((before, *shape), jnp.float32)] if before else []
        parts.append(values)
        if after:
            parts.append(jnp.zeros((after, *shape), jnp.float32))
        return jnp.concatenate(parts, 0)

    def wide(rows):
        return jnp.broadcast_to(rows[:, None, :], (rows.shape[0], 8, 128))

    def shift(inner, outer, step, axis):
        some = inner if inner is not None else outer
        size = some.shape[axis]
        edge = 0 if step == 1 else size - 1
        at_edge = lax.broadcasted_iota(jnp.int32, some.shape, axis) == edge
        a = 0.0 if inner is None else roll(inner, step, axis)
        b = 0.0 if outer is None else roll(outer, step, axis)
        return jnp.where(at_edge, b, a), jnp.where(at_edge, a, b)

    def difference(inner, outer, axis):
        up, down = shift(inner, outer, -1, axis), shift(inner, outer, 1, axis)
        return up[0] - down[0], up[1] - down[1]

    def both_sides(inner, outer, axis):
        up, down = shift(inner, outer, -1, axis), shift(inner, outer, 1, axis)
        return up[0] + down[0], up[1] + down[1]

    def vertical_layers(adj, ref, start):
        for k in range(6):
            ref[start + k] = jnp.where(low, adj[FALLING[k], 8], adj[RISING[k], 1])

    def take_vertical(adj, ref, start):
        for k in range(6):
            layer = ref[start + k]
            adj[RISING[k], 9] = layer
            adj[FALLING[k], 0] = layer

    def edge_row(sign):
        return 0 if sign == 1 else 7

    def rows_x(adj, sign, ref, slot):
        for k, i in enumerate(ALONG_X[sign]):
            cz = VELOCITY[i][0]
            ref[slot, k] = adj[i, 1 + cz : 9 + cz, edge_row(sign), :]

    def pack_y(adj, sign, packed):
        source = 0 if sign == 1 else 127
        for k, i in enumerate(ALONG_Y[sign]):
            cz = VELOCITY[i][0]
            values = roll(adj[i, 1 + cz : 9 + cz], k - source, 2)
            packed = values if packed is None else jnp.where(lane3 == k, values, packed)
        return packed

    def well(value):
        return WELL * value * (value - 1.0) * (value - 0.5)

    def well_slope(value):
        return WELL * (3.0 * value * value - 3.0 * value + 0.5)

    def phase_gradients(which, tile, place):
        full = phase[which]
        ahead, behind = SLOT[(-1, 0)], SLOT[(1, 0)]

        def side(slot):
            near = wide(x1r[slot, tile])
            far = wide(x1r[slot, tile + 1])
            first = x1r[slot, 10, place : place + 1, :]
            last = x1r[slot, 10, place + 1 : place + 2, :]
            first = jnp.broadcast_to(first, (8, 128))[None]
            last = jnp.broadcast_to(last, (8, 128))[None]
            return first, near, far, last

        first_n, near_n, far_n, last_n = side(ahead)
        first_p, near_p, far_p, last_p = side(behind)
        x_mid = jnp.where(
            row3 < 4,
            jnp.where(row3 == 0, near_n, far_n),
            jnp.where(row3 == 7, near_p, far_p),
        )
        upper_half = row[None] < 4
        x_tile = jnp.concatenate(
            [jnp.where(upper_half, first_n, first_p), x_mid, jnp.where(upper_half, last_n, last_p)], 0
        )
        start = 6 + 2 * (1 - which)
        y_tile = jnp.where(
            lanes_of(10) < 64,
            roll(y1r[SLOT[(0, -1)] - 2], -start, 2),
            roll(y1r[SLOT[(0, 1)] - 2], 126 - start, 2),
        )
        t = 1 - which
        before_y, after_y = lane < 64, lane >= 64
        corner_n = jnp.where(before_y, c1r[SLOT[(-1, -1)], t], c1r[SLOT[(-1, 1)], t])
        corner_p = jnp.where(before_y, c1r[SLOT[(1, -1)], t], c1r[SLOT[(1, 1)], t])
        b_tile = jnp.where(row3 < 4, wide(corner_n), wide(corner_p))
        mid, y_mid = full[1:11], y_tile[1:9]
        slope[which, 0] = well_slope(mid)
        slope[which, 1] = well_slope(x_tile)
        slope[which, 2] = well_slope(y_tile)

        x_up, x_down = shift(mid, x_tile, -1, 1), shift(mid, x_tile, 1, 1)
        y_up, y_down = shift(mid, y_tile, -1, 2), shift(mid, y_tile, 1, 2)
        grads[which, 0] = 0.5 * (full[3:11] - full[1:9])
        grads[which, 1] = 0.5 * (x_up[0] - x_down[0])[1:9]
        grads[which, 2] = 0.5 * (y_up[0] - y_down[0])[1:9]
        lap = x_up[0] + x_down[0] + y_up[0] + y_down[0] + full[:10] + full[2:] - 6.0 * mid
        pot = well(mid) - STIFFNESS * lap
        pot = jnp.concatenate(
            [jnp.where(low, 0.0, pot[:1]), pot[1:9], jnp.where(low, pot[9:], 0.0)], 0
        )
        lap = (x_up[1] + x_down[1])[1:9] + both_sides(x_mid, b_tile, 2)[0]
        lap = lap + x_tile[:8] + x_tile[2:] - 6.0 * x_mid
        pot_x = well(x_mid) - STIFFNESS * lap
        lap = (y_up[1] + y_down[1])[1:9] + both_sides(y_mid, b_tile, 1)[0]
        lap = lap + y_tile[:8] + y_tile[2:] - 6.0 * y_mid
        pot_y = well(y_mid) - STIFFNESS * lap
        grads[which, 3] = 0.5 * (pot[2:] - pot[:8])
        grads[which, 4] = 0.5 * difference(pot[1:9], pot_x, 1)[0]
        grads[which, 5] = 0.5 * difference(pot[1:9], pot_y, 2)[0]

    def total(values):
        values = list(values)
        while len(values) > 1:
            values = [
                values[j] + values[j + 1] if j + 1 < len(values) else values[j]
                for j in range(0, len(values), 2)
            ]
        return values[0]

    def signed(values, weight):
        plus = [values[i] for i in range(len(values)) if weight(i) == 1]
        minus = [values[i] for i in range(len(values)) if weight(i) == -1]
        return total(plus) - total(minus)

    def part(d):
        return lambda i: VELOCITY[i][d]

    def pair(d, e):
        return lambda i: VELOCITY[i][d] * VELOCITY[i][e]

    def dot(u, v):
        return u[0] * v[0] + u[1] * v[1] + u[2] * v[2]

    def flow_moments(which):
        def layer(z, carry):
            f = [pops[which][i, z].astype(jnp.float32) for i in range(19)]
            flow[which, 0, z] = total(f)
            for d in range(3):
                flow[which, 1 + d, z] = signed(f, part(d))
            return carry

        lax.fori_loop(0, 8, layer, 0)

    def bounce(z, i, own, bounced):
        if VELOCITY[i][0] == 1:
            return jnp.where(jnp.logical_and(z == 7, jnp.logical_not(low)), bounced, own)
        if VELOCITY[i][0] == -1:
            return jnp.where(jnp.logical_and(z == 0, low), bounced, own)
        return own

    def arrived(z, i, adj, xr, yr, ystart, cr, tile):
        cz, cx, cy = VELOCITY[i]
        own = adj[i, z + (1 + cz)]
        erow = 7 if cx == 1 else 0
        elane = 127 if cy == 1 else 0
        moved = own
        if cx:
            k = ALONG_X[cx].index(i)
            got = jnp.broadcast_to(xr[SLOT[(-cx, 0)], k, pl.ds(z, 1), :], (8, 128))
            moved = jnp.where(row == erow, got, roll(own, -cx, 0))
        if cy:
            k = ALONG_Y[cy].index(i)
            got = roll(yr[SLOT[(0, -cy)] - 2, ystart + z], elane - k, 1)
            if cx:
                corner = cr[SLOT[(-cx, -cy)], tile, pl.ds(z, 1), :]
                corner = roll(jnp.broadcast_to(corner, (8, 128)), -cy, 1)
                got = jnp.where(row == erow, corner, roll(got, -cx, 0))
            moved = jnp.where(lane == elane, got, roll(moved, -cy, 1))
        return bounce(z, i, moved, adj[OPPOSITE[i], z + 1])

    PAIRS = [(0, 0), (1, 1), (2, 2), (1, 0), (2, 0), (2, 1)]

    def gather_flow(which, *sources):
        def layer(z, carry):
            a = [arrived(z, i, *sources) for i in range(19)]
            for i in range(19):
                arrive_f[i, z] = a[i]
            wa = [a[0] * (1.0 / 3.0)]
            wa += [a[i] * (1.0 / 18.0) for i in range(1, 7)]
            wa += [a[i] * (1.0 / 36.0) for i in range(7, 19)]
            moments[0, z] = total(wa)
            for d in range(3):
                moments[1 + d, z] = signed(wa, part(d))
            for n, (d, e) in enumerate(PAIRS):
                if d == e:
                    moments[4 + n, z] = total([wa[i] for i in range(19) if VELOCITY[i][d]])
                else:
                    moments[4 + n, z] = signed(wa, pair(d, e))
            moments[10, z] = total([a[i] * pops[which][i, z].astype(jnp.float32) for i in range(19)])
            return carry

        lax.fori_loop(0, 8, layer, 0)

    def collide_adjoint(which, sources, result, offset, with_phi):
        def layer(z, carry):
            def arrived_phi(i):
                cz, cx, cy = VELOCITY[i]
                own = phi[z + (1 + cz)]
                if cx:
                    erow = 7 if cx == 1 else 0
                    got = jnp.broadcast_to(x3r[SLOT[(-cx, 0)], pl.ds(z, 1), :], (8, 128))
                    own = jnp.where(row == erow, got, roll(own, -cx, 0))
                if cy:
                    elane = 127 if cy == 1 else 0
                    got = roll(y3r[SLOT[(0, -cy)] - 2, z], -cy, 1)
                    own = jnp.where(lane == elane, got, roll(own, -cy, 1))
                return bounce(z, i, own, phi[z + 1])

            g = [arrived(z, i, *sources) for i in range(19, 26)]
            if with_phi:
                g = [g[k] + arrived_phi(19 + k) for k in range(7)]
            frac = phase[which, z + 2]
            pressure = flow[which, 0, z]
            momentum = [flow[which, 1 + d, z] for d in range(3)]
            a0 = moments[0, z]
            a1 = [moments[1 + d, z] for d in range(3)]
            a2 = {}
            for n, (d, e) in enumerate(PAIRS):
                a2[d, e] = a2[e, d] = moments[4 + n, z]
            af = moments[10, z]
            b0 = 0.25 * g[0] + 0.125 * total(g[1:])
            b1 = [0.125 * (g[1 + 2 * d] - g[2 + 2 * d]) for d in range(3)]
            density = 0.2 + 0.8 * frac
            rate = 1.1 + 0.5 * frac
            half = 1.0 - 0.5 * rate
            pg = [grads[which, d, z] for d in range(3)]
            mg = [grads[which, 3 + d, z] for d in range(3)]
            force = [-frac * m for m in mg]
            inverse = 1.0 / density
            u = [(momentum[d] + 0.5 * force[d]) * inverse for d in range(3)]
            a2u = [dot([a2[d, e] for e in range(3)], u) for d in range(3)]
            a2f = [dot([a2[d, e] for e in range(3)], force) for d in range(3)]
            speed = dot(u, u)
            quad = 3.0 * dot(u, a1) + 4.5 * dot(u, a2u) - 1.5 * speed * a0
            slant = [3.0 * a1[d] - 3.0 * a0 * u[d] + 9.0 * a2u[d] for d in range(3)]
            rate_density = rate * density
            phase_pull = (4.0 * PHASE_RATE) * frac
            ubar = [
                rate_density * slant[d]
                + half * (9.0 * a2f[d] - 3.0 * a0 * force[d])
                + phase_pull * b1[d]
                for d in range(3)
            ]
            jbar = [ubar[d] * inverse for d in range(3)]
            fbar = [half * slant[d] + 0.5 * jbar[d] for d in range(3)]
            density_bar = rate * quad - dot(jbar, u)
            rate_bar = pressure * a0 + density * quad - af - 0.5 * dot(force, slant)
            imag = lax.rsqrt(dot(pg, pg) + 0.0625)
            normal = [p * imag for p in pg]
            nb1 = dot(normal, b1)
            frac_bar = (
                0.5 * rate_bar
                + 0.8 * density_bar
                - dot(mg, fbar)
                + PHASE_RATE * (b0 + 4.0 * dot(u, b1))
                + (PHASE_RATE * 4.0 * SHARPEN) * (1.0 - 2.0 * frac) * nb1
            )
            pull = (PHASE_RATE * 4.0 * SHARPEN) * frac * (1.0 - frac) * imag
            for d in range(3):
                sens[d, z] = pull * (b1[d] - normal[d] * nb1)
                sens[3 + d, z] = -frac * fbar[d]
            phibar[z] = frac_bar
            pbar = rate * a0
            keep = 1.0 - rate
            for i in range(19):
                value = keep * arrive_f[i, z] + pbar
                for d in range(3):
                    if VELOCITY[i][d] == 1:
                        value = value + jbar[d]
                    elif VELOCITY[i][d] == -1:
                        value = value - jbar[d]
                result[i, z + offset] = value
            for k in range(7):
                result[19 + k, z + offset] = (1.0 - PHASE_RATE) * g[k]
            return carry

        lax.fori_loop(0, 8, layer, 0)

    def phase_share(which):
        def spread(first):
            vz = sens[first]
            in_x, out_x = difference(sens[first + 1], None, 1)
            in_y, out_y = difference(sens[first + 2], None, 2)
            inner = layers(-0.5 * (in_x + in_y), 1, 1)
            inner = inner + 0.5 * (layers(vz, 2, 0) - layers(vz, 0, 2))
            return inner, layers(-0.5 * out_x, 1, 1), layers(-0.5 * out_y, 1, 1)

        mu, mu_x, mu_y = spread(3)
        mu = jnp.concatenate(
            [jnp.where(low, 0.0, mu[:1]), mu[1:9], jnp.where(low, mu[9:], 0.0)], 0
        )
        own, own_x, own_y = spread(0)
        in_x, out_x = both_sides(mu, mu_x, 1)
        in_y, out_y = both_sides(mu, mu_y, 2)
        over_x, corner_x = both_sides(mu_x[1:9], None, 2)
        over_y, corner_y = both_sides(mu_y[1:9], None, 1)
        inner = slope[which, 0] * mu - STIFFNESS * (in_x + in_y - 6.0 * mu) + own
        inner = inner + layers(phibar[...], 1, 1)
        inner = layers(inner, 1, 1) - STIFFNESS * (layers(mu, 2, 0) + layers(mu, 0, 2))

        def beside(scale, values, out_share, over, extra):
            vertical = layers(values[1:], 0, 1) + layers(values[:9], 1, 0)
            lap = out_share + layers(over, 1, 1) + vertical - 6.0 * values
            return scale * values - STIFFNESS * lap + extra

        side_x = beside(slope[which, 1], mu_x, out_x, over_x, own_x)
        side_y = beside(slope[which, 2], mu_y, out_y, over_y, own_y)
        return inner, side_x, side_y, -STIFFNESS * (corner_x + corner_y)

    def send_share(share, zs, zr):
        inner, side_x, side_y, _ = share
        zs[:2] = jnp.where(low, inner[10:], inner[:2])
        zs[2:3] = jnp.where(low, side_x[9:], side_x[:1])
        zs[3:4] = jnp.where(low, side_y[9:], side_y[:1])
        return send(zs, zr, partner)

    def share_sides(share, zcopy, zr, xs, xr, ys, yr, cs, cr):
        inner, side_x, side_y, corner = share
        zcopy.wait_recv()

        def merge(values, extra, count):
            lower = values[:count] + jnp.where(low, 0.0, extra)
            upper = values[8 - count :] + jnp.where(low, extra, 0.0)
            return jnp.concatenate([lower, values[count : 8 - count], upper], 0)

        group = []
        ys[...] = merge(side_y[1:9], zr[3:4], 1)
        for way in SIDES[2:]:
            slot = SLOT[way] - 2
            group.append(send(ys, yr.at[slot], device(way)))
        side_x = merge(side_x[1:9], zr[2:3], 1)
        xs[0, 0], xs[0, 1] = side_x[:, 7, :], side_x[:, 6, :]
        xs[1, 0], xs[1, 1] = side_x[:, 0, :], side_x[:, 1, :]
        cs[0], cs[1] = corner[:, 7, :], corner[:, 0, :]
        for way in CORNERS:
            group.append(send(cs.at[0 if way[0] < 0 else 1], cr.at[SLOT[way]], device(way)))
        for way in SIDES[:2]:
            slot = SLOT[way]
            group.append(send(xs.at[slot], xr.at[slot], device(way)))
        return merge(inner[2:10], zr[:2], 2), group

    def collect_share(center, group, xr, yr, cr):
        arrive(group)
        prev, after = SLOT[(1, 0)], SLOT[(-1, 0)]
        near = jnp.where(row3 < 4, wide(xr[prev, 0]), wide(xr[after, 0]))
        far = jnp.where(row3 < 4, wide(xr[prev, 1]), wide(xr[after, 1]))
        end = jnp.logical_or(row3 == 0, row3 == 7)
        next_end = jnp.logical_or(row3 == 1, row3 == 6)
        result = center + jnp.where(end, near, jnp.where(next_end, far, 0.0))
        from_y = jnp.where(lane3 < 64, yr[SLOT[(0, 1)] - 2], yr[SLOT[(0, -1)] - 2])
        result = result + jnp.where(jnp.logical_or(lane3 < 2, lane3 >= 126), from_y, 0.0)
        before = lane < 64
        ends = jnp.logical_or(lane == 0, lane == 127)
        prev_c = jnp.where(ends, jnp.where(before, cr[SLOT[(1, 1)]], cr[SLOT[(1, -1)]]), 0.0)
        next_c = jnp.where(ends, jnp.where(before, cr[SLOT[(-1, 1)]], cr[SLOT[(-1, -1)]]), 0.0)
        corners = jnp.where(row3 == 0, wide(prev_c), wide(next_c))
        return result + jnp.where(end, corners, 0.0)

    for copy in load_phase:
        copy.wait()
    for which in range(2):
        phase[which, 2:10] = total([pops[which][i].astype(jnp.float32) for i in range(19, 26)])
        z1s[2 * which : 2 * which + 2] = jnp.where(low, phase[which, 8:10], phase[which, 2:4])
    for copy in load_cot:
        copy.wait()
    vertical_layers(adj_a, z1s, 4)
    pl.semaphore_wait(barrier, 9)
    vertical = send(z1s, z1r, partner)
    for copy in load_flow:
        copy.wait()
    flow_moments(1)
    vertical.wait_recv()
    for which in range(2):
        got = z1r[2 * which : 2 * which + 2]
        phase[which, :2] = jnp.where(low, 0.0, got)
        phase[which, 10:] = jnp.where(low, got, 0.0)
    take_vertical(adj_a, z1r, 4)

    first = []
    for way in SIDES[2:]:
        slot = SLOT[way] - 2
        source = 0 if way[1] < 0 else 126
        packed = jnp.where(
            lanes_of(10) < 8,
            roll(phase[1, 1:11], 6 - source, 2),
            roll(phase[0, 1:11], 8 - source, 2),
        )
        y1s[slot, 0] = packed[0]
        y1s[slot, 9] = packed[9]
        middle = packed[1:9]
        entries = pack_y(adj_a, -way[1], None)
        y1s[slot, 1:9] = jnp.where(lane3 < 6, entries, middle)
        first.append(send(y1s.at[slot], y1r.at[slot], device(way)))
    for way in CORNERS:
        slot = SLOT[way]
        r = edge_row(-way[0])
        c1s[slot, 0] = phase[1, 2:10, r, :]
        c1s[slot, 1] = phase[0, 2:10, r, :]
        c1s[slot, 2] = adj_a[DIAGONAL[(-way[0], -way[1])], 1:9, r, :]
        first.append(send(c1s.at[slot], c1r.at[slot], device(way)))
    for way in SIDES[:2]:
        slot = SLOT[way]
        r = edge_row(-way[0])
        rows_x(adj_a, -way[0], x1s, slot)
        for n, which in enumerate((1, 0)):
            x1s[slot, 6 + 2 * n] = phase[which, 2:10, r, :]
            x1s[slot, 7 + 2 * n] = phase[which, 2:10, r + (1 if r == 0 else -1), :]
            x1s[slot, 10, 2 * n : 2 * n + 1, :] = phase[which, 1, r : r + 1, :]
            x1s[slot, 10, 2 * n + 1 : 2 * n + 2, :] = phase[which, 10, r : r + 1, :]
        x1s[slot, 10, 4:, :] = jnp.zeros((4, 128), jnp.float32)
        first.append(send(x1s.at[slot], x1r.at[slot], device(way)))
    flow_moments(0)
    arrive(first)
    sources = (adj_a, x1r, y1r, 1, c1r, 2)
    phase_gradients(1, 6, 0)
    gather_flow(1, *sources)
    collide_adjoint(1, sources, adj_b, 1, False)

    vertical_layers(adj_b, z2s, 0)
    vertical = send(z2s, z2r, partner)
    share = phase_share(1)
    zcopy = send_share(share, zd2s, zd2r)
    phase_gradients(0, 8, 2)
    center, group = share_sides(share, zcopy, zd2r, xd2s, xd2r, yd2s, yd2r, cd2s, cd2r)
    vertical.wait_recv()
    take_vertical(adj_b, z2r, 0)
    second = []
    for way in SIDES[2:]:
        slot = SLOT[way] - 2
        y2s[slot] = pack_y(adj_b, -way[1], None)
        second.append(send(y2s.at[slot], y2r.at[slot], device(way)))
    for way in CORNERS:
        slot = SLOT[way]
        c2s[slot, 0] = adj_b[DIAGONAL[(-way[0], -way[1])], 1:9, edge_row(-way[0]), :]
        second.append(send(c2s.at[slot], c2r.at[slot], device(way)))
    for way in SIDES[:2]:
        slot = SLOT[way]
        rows_x(adj_b, -way[0], x2s, slot)
        second.append(send(x2s.at[slot], x2r.at[slot], device(way)))
    phi[1:9] = collect_share(center, group, xd2r, yd2r, cd2r)
    third = []
    for way in SIDES:
        slot = SLOT[way]
        if way[0]:
            x3s[slot] = phi[1:9, edge_row(-way[0]), :]
            third.append(send(x3s.at[slot], x3r.at[slot], device(way)))
        else:
            third.append(send(phi.at[pl.ds(1, 8)], y3r.at[slot - 2], device(way)))
    z3s[...] = jnp.where(low, phi[8], phi[1])
    third.append(send(z3s, z3r, partner))
    arrive(second)
    sources = (adj_b, x2r, y2r, 0, c2r, 0)
    gather_flow(0, *sources)
    arrive(third)
    phi[0] = z3r[...]
    phi[9] = z3r[...]
    collide_adjoint(0, sources, out, 0, True)

    share = phase_share(0)
    zcopy = send_share(share, zd4s, zd4r)
    center, group = share_sides(share, zcopy, zd4r, xd4s, xd4r, yd4s, yd4r, cd4s, cd4r)
    last = collect_share(center, group, xd4r, yd4r, cd4r)
    for k in range(7):
        out[19 + k] = out[19 + k] + last
    for copy in copies:
        copy.wait_send()


def local(populations0, populations1, cotangent):
    def vmem(*shape):
        return pltpu.VMEM(shape + (8, 128), jnp.float32)

    share = [
        vmem(4), vmem(4), vmem(2, 2), vmem(2, 2),
        vmem(8), vmem(2, 8), vmem(2), vmem(4),
    ]
    scratch = [
        pltpu.VMEM(populations0.shape, populations0.dtype),
        pltpu.VMEM(populations1.shape, populations1.dtype),
        vmem(26, 10), vmem(26, 10), vmem(2, 12), vmem(2, 6, 8), vmem(6, 8), vmem(8),
        vmem(2, 3, 10), vmem(10), vmem(2, 4, 8), vmem(11, 8), vmem(19, 8),
        vmem(10), vmem(10), vmem(2, 11), vmem(2, 11), vmem(2, 10), vmem(2, 10), vmem(4, 3), vmem(4, 3),
        vmem(6), vmem(6), vmem(2, 6), vmem(2, 6), vmem(2, 8), vmem(2, 8), vmem(4, 1), vmem(4, 1),
        *share,
        vmem(), vmem(), vmem(2), vmem(2), vmem(2, 8),
        *share,
        pltpu.SemaphoreType.DMA((48,)),
        pltpu.SemaphoreType.DMA((48,)),
        pltpu.SemaphoreType.DMA((6,)),
    ]
    return pl.pallas_call(
        kernel,
        out_shape=jax.ShapeDtypeStruct(cotangent.shape, jnp.float32),
        in_specs=[pl.BlockSpec(memory_space=pltpu.HBM)] * 3,
        out_specs=pl.BlockSpec(memory_space=pltpu.VMEM),
        scratch_shapes=scratch,
        compiler_params=pltpu.CompilerParams(
            collective_id=0, has_side_effects=True, vmem_limit_bytes=40 * 1024 * 1024
        ),
    )(populations0, populations1, cotangent)


def solution(mesh):
    spec = P(None, "gz", "gx", "gy")
    return jax.shard_map(
        local, mesh=mesh, in_specs=(spec, spec, spec), out_specs=spec, check_vma=False
    )
```

time: 38.6 us -> 35.1 us (0.909)
  Pallas kernels: 34.3 us -> 30.7 us
    pallas_call x1, Pallas kernels: 34.3 us -> 30.7 us  [local(): pl.pallas_call(kernel, out_shape=jax.ShapeDtypeStruct(cotangent.shape, jn...]
where the time goes in v2:
time: 35.1 us; the launch traced here: 34.8 us
  Pallas kernels  30.7 us (87%)
  local copies, waits for them, and re-layouts  4.07 us (12%)
    pallas_call x1, Pallas kernels, local(): pl.pallas_call(kernel, out_shape=jax.ShapeDtypeStruct(cotangent.shape, jn...  30.7 us
    unnamed x7, local copies, waits for them, and re-layouts  4.07 us

profile of v2, /device:TPU:0, one launch (start us, length us, event | category | flops | bytes accessed | tf_op | source)
XLA Modules:
  0.0 34.8 jit_solution(2739383861357090843)
XLA Ops:
  0.0 0.0 copy-start
  0.0 1.2 %copy-done = f32[26,8,8,128]{3,2,1,0:T(8,128)S(1)} copy-done((f32[26,8,8,128]{3,2,1,0:T(8,128)S(1)}, f32[26,8,8,128]{3,2,1,0:T(8,128)}, u32[]{:S(2)}) %copy-start) | copy-done | bytes 851992
  1.2 0.0 copy-start.1
  1.2 1.0 %copy-done.1 = bf16[26,8,8,128]{3,2,1,0:T(8,128)(2,1)S(1)} copy-done((bf16[26,8,8,128]{3,2,1,0:T(8,128)(2,1)S(1)}, bf16[26,8,8,128]{3,2,1,0:T(8,128)(2,1)}, u32[]{:S(2)}) %copy-start.1) | copy-done | bytes 426008
  2.2 0.0 copy-start.2
  2.2 1.0 %copy-done.2 = bf16[26,8,8,128]{3,2,1,0:T(8,128)(2,1)S(1)} copy-done((bf16[26,8,8,128]{3,2,1,0:T(8,128)(2,1)S(1)}, bf16[26,8,8,128]{3,2,1,0:T(8,128)(2,1)}, u32[]{:S(2)}) %copy-start.2) | copy-done | bytes 426008
  3.2 30.7 %shard_map.37 = f32[26,8,8,128]{3,2,1,0:T(8,128)S(1)} custom-call(bf16[26,8,8,128]{3,2,1,0:T(8,128)(2,1)S(1)} %copy-done.1, bf16[26,8,8,128]{3,2,1,0:T(8,128)(2,1)S(1)} %copy-done.2, f32[26,8,8,128]{3,2,1,0:T(8,128)S(1)} %copy-done), custom_call_target="tpu_custom_call" | custom-call | tf_op jit(solution)/shard_map/pallas_call | solution.py:626
  33.9 0.9 %copy.5 = f32[26,8,8,128]{3,2,1,0:T(8,128)} copy(f32[26,8,8,128]{3,2,1,0:T(8,128)S(1)} %shard_map.37) | data formatting | bytes 1703936
Async XLA Ops:
  0.0 1.2 %copy-start = (f32[26,8,8,128]{3,2,1,0:T(8,128)S(1)}, f32[26,8,8,128]{3,2,1,0:T(8,128)}, u32[]{:S(2)}) copy-start(f32[26,8,8,128]{3,2,1,0:T(8,128)} %cot_hbm.1) | copy-start | bytes 2555908
  1.2 1.0 %copy-start.1 = (bf16[26,8,8,128]{3,2,1,0:T(8,128)(2,1)S(1)}, bf16[26,8,8,128]{3,2,1,0:T(8,128)(2,1)}, u32[]{:S(2)}) copy-start(bf16[26,8,8,128]{3,2,1,0:T(8,128)(2,1)} %pop0_hbm.1) | copy-start | bytes 1277956
  2.2 1.0 %copy-start.2 = (bf16[26,8,8,128]{3,2,1,0:T(8,128)(2,1)S(1)}, bf16[26,8,8,128]{3,2,1,0:T(8,128)(2,1)}, u32[]{:S(2)}) copy-start(bf16[26,8,8,128]{3,2,1,0:T(8,128)(2,1)} %pop1_hbm.1) | copy-start | bytes 1277956

commit v3 on v2

--- a/solution.py
+++ b/solution.py
@@ -48,8 +48,8 @@
 
 
 def kernel(
-    pop0_hbm, pop1_hbm, cot_hbm, out,
-    pop0, pop1, adj_a, adj_b, phase, grads, sens, phibar, slope, phi, flow, moments, arrive_f,
+    pop0_hbm, pop1_hbm, cot_hbm, out_hbm,
+    out, pop0, pop1, adj_a, adj_b, phase, grads, sens, phibar, slope, phi, flow, moments, arrive_f,
     z1s, z1r, x1s, x1r, y1s, y1r, c1s, c1r,
     z2s, z2r, x2s, x2r, y2s, y2r, c2s, c2r,
     zd2s, zd2r, xd2s, xd2r, yd2s, yd2r, cd2s, cd2r,
@@ -591,12 +591,19 @@
     phi[9] = z3r[...]
     collide_adjoint(0, sources, out, 0, True)
 
+    stores = [
+        load(out.at[pl.ds(0, 10)], out_hbm.at[pl.ds(0, 10)], 6),
+        load(out.at[pl.ds(10, 9)], out_hbm.at[pl.ds(10, 9)], 7),
+    ]
     share = phase_share(0)
     zcopy = send_share(share, zd4s, zd4r)
     center, group = share_sides(share, zcopy, zd4r, xd4s, xd4r, yd4s, yd4r, cd4s, cd4r)
     last = collect_share(center, group, xd4r, yd4r, cd4r)
     for k in range(7):
         out[19 + k] = out[19 + k] + last
+    stores.append(load(out.at[pl.ds(19, 7)], out_hbm.at[pl.ds(19, 7)], 8))
+    for copy in stores:
+        copy.wait()
     for copy in copies:
         copy.wait_send()
 
@@ -610,6 +617,7 @@
         vmem(8), vmem(2, 8), vmem(2), vmem(4),
     ]
     scratch = [
+        vmem(26, 8),
         pltpu.VMEM(populations0.shape, populations0.dtype),
         pltpu.VMEM(populations1.shape, populations1.dtype),
         vmem(26, 10), vmem(26, 10), vmem(2, 12), vmem(2, 6, 8), vmem(6, 8), vmem(8),
@@ -621,16 +629,16 @@
         *share,
         pltpu.SemaphoreType.DMA((48,)),
         pltpu.SemaphoreType.DMA((48,)),
-        pltpu.SemaphoreType.DMA((6,)),
+        pltpu.SemaphoreType.DMA((9,)),
     ]
     return pl.pallas_call(
         kernel,
         out_shape=jax.ShapeDtypeStruct(cotangent.shape, jnp.float32),
         in_specs=[pl.BlockSpec(memory_space=pltpu.HBM)] * 3,
-        out_specs=pl.BlockSpec(memory_space=pltpu.VMEM),
+        out_specs=pl.BlockSpec(memory_space=pltpu.HBM),
         scratch_shapes=scratch,
         compiler_params=pltpu.CompilerParams(
-            collective_id=0, has_side_effects=True, vmem_limit_bytes=40 * 1024 * 1024
+            collective_id=0, has_side_effects=True, vmem_limit_bytes=60 * 1024 * 1024
         ),
     )(populations0, populations1, cotangent)
 

time: 35.1 us -> 33.3 us (0.949)
  local copies, waits for them, and re-layouts: 4.07 us -> 2.14 us
    unnamed x7 -> x1, local copies, waits for them, and re-layouts: 4.07 us -> 2.14 us
where the time goes in v3:
time: 33.3 us; the launch traced here: 33.1 us
  Pallas kernels  30.9 us (93%)
  local copies, waits for them, and re-layouts  2.14 us (6%)
    pallas_call x1, Pallas kernels, local(): pl.pallas_call(kernel, out_shape=jax.ShapeDtypeStruct(cotangent.shape, jn...  30.9 us
    unnamed x1, local copies, waits for them, and re-layouts  2.14 us

profile of v3, /device:TPU:0, one launch (start us, length us, event | category | flops | bytes accessed | tf_op | source)
XLA Modules:
  0.0 33.1 jit_solution(12977596950785407072)
XLA Ops:
  0.0 30.9 %shard_map.37 = f32[26,8,8,128]{3,2,1,0:T(8,128)} custom-call(bf16[26,8,8,128]{3,2,1,0:T(8,128)(2,1)} %pop0_hbm.1, bf16[26,8,8,128]{3,2,1,0:T(8,128)(2,1)} %pop1_hbm.1, f32[26,8,8,128]{3,2,1,0:T(8,128)} %cot_hbm.1), custom_call_target="tpu_custom_call" | custom-call | tf_op jit(solution)/shard_map/pallas_call | solution.py:634
  31.0 2.1 %copy.5 = f32[26,8,8,128]{3,2,1,0:T(8,128)} copy(f32[26,8,8,128]{3,2,1,0:T(8,128)} %shard_map.37) | data formatting | bytes 1703936

commit v4 on v3

--- a/solution.py
+++ b/solution.py
@@ -631,16 +631,20 @@
         pltpu.SemaphoreType.DMA((48,)),
         pltpu.SemaphoreType.DMA((9,)),
     ]
+    operands = [
+        pltpu.with_memory_space_constraint(operand, pltpu.HBM)
+        for operand in (populations0, populations1, cotangent)
+    ]
     return pl.pallas_call(
         kernel,
         out_shape=jax.ShapeDtypeStruct(cotangent.shape, jnp.float32),
         in_specs=[pl.BlockSpec(memory_space=pltpu.HBM)] * 3,
-        out_specs=pl.BlockSpec(memory_space=pltpu.HBM),
+        out_specs=pl.BlockSpec(memory_space=pl.ANY),
         scratch_shapes=scratch,
         compiler_params=pltpu.CompilerParams(
-            collective_id=0, has_side_effects=True, vmem_limit_bytes=60 * 1024 * 1024
+            collective_id=0, has_side_effects=True, vmem_limit_bytes=40 * 1024 * 1024
         ),
-    )(populations0, populations1, cotangent)
+    )(*operands)
 
 
 def solution(mesh):

time: 33.3 us -> 31.9 us (0.958)
  local copies, waits for them, and re-layouts: 2.14 us -> 0.9 us
    unnamed x1, local copies, waits for them, and re-layouts: 2.14 us -> 0.9 us
where the time goes in v4:
time: 31.9 us; the launch traced here: 31.7 us
  Pallas kernels  30.8 us (97%)
  local copies, waits for them, and re-layouts  0.9 us (3%)
    pallas_call x1, Pallas kernels, local(): pl.pallas_call(kernel, out_shape=jax.ShapeDtypeStruct(cotangent.shape, jn...  30.8 us
    unnamed x1, local copies, waits for them, and re-layouts  0.9 us

profile of v4, /device:TPU:0, one launch (start us, length us, event | category | flops | bytes accessed | tf_op | source)
XLA Modules:
  0.0 31.7 jit_solution(16398114815100420395)
XLA Ops:
  0.0 30.8 %shard_map.37 = f32[26,8,8,128]{3,2,1,0:T(8,128)S(1)} custom-call(bf16[26,8,8,128]{3,2,1,0:T(8,128)(2,1)} %pop0_hbm.1, bf16[26,8,8,128]{3,2,1,0:T(8,128)(2,1)} %pop1_hbm.1, f32[26,8,8,128]{3,2,1,0:T(8,128)} %cot_hbm.1), custom_call_target="tpu_custom_call" | custom-call | tf_op jit(solution)/shard_map/pallas_call | solution.py:638
  30.8 0.9 %copy.5 = f32[26,8,8,128]{3,2,1,0:T(8,128)} copy(f32[26,8,8,128]{3,2,1,0:T(8,128)S(1)} %shard_map.37) | data formatting | bytes 1703936

commit v5 on v4

--- a/solution.py
+++ b/solution.py
@@ -52,9 +52,10 @@
     out, pop0, pop1, adj_a, adj_b, phase, grads, sens, phibar, slope, phi, flow, moments, arrive_f,
     z1s, z1r, x1s, x1r, y1s, y1r, c1s, c1r,
     z2s, z2r, x2s, x2r, y2s, y2r, c2s, c2r,
-    zd2s, zd2r, xd2s, xd2r, yd2s, yd2r, cd2s, cd2r,
+    zx1s, zx1r, zy1s, zy1r,
+    zd2s, zd2r, zs2s, zs2r, xd2s, xd2r, yd2s, yd2r, cd2s, cd2r,
     z3s, z3r, x3s, x3r, y3r,
-    zd4s, zd4r, xd4s, xd4r, yd4s, yd4r, cd4s, cd4r,
+    zd4s, zd4r, zs4s, zs4r, xd4s, xd4r, yd4s, yd4r, cd4s, cd4r,
     send_sem, recv_sem, load_sem,
 ):
     gx, gy, gz = lax.axis_index("gx"), lax.axis_index("gy"), lax.axis_index("gz")
@@ -84,8 +85,12 @@
     def device(way):
         return (lax.rem(gx + way[0] + nx, nx), lax.rem(gy + way[1] + ny, ny), gz)
 
+    def across(way):
+        return (*device(way)[:2], 1 - gz)
+
     barrier = pltpu.get_barrier_semaphore()
-    for target in [partner] + [device(way) for way in SIDES + CORNERS]:
+    others = [across(way) for way in SIDES]
+    for target in [partner] + others + [device(way) for way in SIDES + CORNERS]:
         pl.semaphore_signal(barrier, inc=1, device_id=target, device_id_type=MESH)
 
     copies = []
@@ -160,6 +165,11 @@
             layer = ref[start + k]
             adj[RISING[k], 9] = layer
             adj[FALLING[k], 0] = layer
+
+    def slanted(sign, d):
+        rise = [i for i in RISING if VELOCITY[i][d] == sign][0]
+        fall = [i for i in FALLING if VELOCITY[i][d] == sign][0]
+        return rise, fall
 
     def edge_row(sign):
         return 0 if sign == 1 else 7
@@ -442,40 +452,41 @@
         side_y = beside(slope[which, 2], mu_y, out_y, over_y, own_y)
         return inner, side_x, side_y, -STIFFNESS * (corner_x + corner_y)
 
-    def send_share(share, zs, zr):
-        inner, side_x, side_y, _ = share
-        zs[:2] = jnp.where(low, inner[10:], inner[:2])
-        zs[2:3] = jnp.where(low, side_x[9:], side_x[:1])
-        zs[3:4] = jnp.where(low, side_y[9:], side_y[:1])
-        return send(zs, zr, partner)
-
-    def share_sides(share, zcopy, zr, xs, xr, ys, yr, cs, cr):
+    def send_share(share, zs, zr, es, er, xs, xr, ys, yr, cs, cr):
         inner, side_x, side_y, corner = share
-        zcopy.wait_recv()
-
-        def merge(values, extra, count):
-            lower = values[:count] + jnp.where(low, 0.0, extra)
-            upper = values[8 - count :] + jnp.where(low, extra, 0.0)
-            return jnp.concatenate([lower, values[count : 8 - count], upper], 0)
-
         group = []
-        ys[...] = merge(side_y[1:9], zr[3:4], 1)
+        ys[...] = side_y[1:9]
         for way in SIDES[2:]:
             slot = SLOT[way] - 2
             group.append(send(ys, yr.at[slot], device(way)))
-        side_x = merge(side_x[1:9], zr[2:3], 1)
-        xs[0, 0], xs[0, 1] = side_x[:, 7, :], side_x[:, 6, :]
-        xs[1, 0], xs[1, 1] = side_x[:, 0, :], side_x[:, 1, :]
+        xs[0, 0], xs[0, 1] = side_x[1:9, 7, :], side_x[1:9, 6, :]
+        xs[1, 0], xs[1, 1] = side_x[1:9, 0, :], side_x[1:9, 1, :]
         cs[0], cs[1] = corner[:, 7, :], corner[:, 0, :]
         for way in CORNERS:
             group.append(send(cs.at[0 if way[0] < 0 else 1], cr.at[SLOT[way]], device(way)))
         for way in SIDES[:2]:
             slot = SLOT[way]
             group.append(send(xs.at[slot], xr.at[slot], device(way)))
-        return merge(inner[2:10], zr[:2], 2), group
-
-    def collect_share(center, group, xr, yr, cr):
+        es[0] = jnp.where(low, side_x[9], side_x[0])
+        es[1] = jnp.where(low, side_y[9], side_y[0])
+        for way in SIDES:
+            slot = SLOT[way]
+            group.append(send(es.at[0 if way[0] else 1], er.at[slot], across(way)))
+        zs[...] = jnp.where(low, inner[10:], inner[:2])
+        group.append(send(zs, zr, partner))
+        return inner[2:10], group
+
+    def collect_share(center, group, zr, er, xr, yr, cr):
         arrive(group)
+        prev_x, next_x, prev_y, next_y = (er[SLOT[way]] for way in ((1, 0), (-1, 0), (0, 1), (0, -1)))
+        beyond = jnp.where(row == 0, prev_x, jnp.where(row == 7, next_x, 0.0))
+        beyond = beyond + jnp.where(lane == 0, prev_y, jnp.where(lane == 127, next_y, 0.0))
+        extra = zr[...]
+        to_low = jnp.concatenate([extra[:1], extra[1:] + beyond[None]], 0)
+        to_high = jnp.concatenate([extra[:1] + beyond[None], extra[1:]], 0)
+        lower = center[:2] + jnp.where(low, 0.0, to_high)
+        upper = center[6:] + jnp.where(low, to_low, 0.0)
+        center = jnp.concatenate([lower, center[2:6], upper], 0)
         prev, after = SLOT[(1, 0)], SLOT[(-1, 0)]
         near = jnp.where(row3 < 4, wide(xr[prev, 0]), wide(xr[after, 0]))
         far = jnp.where(row3 < 4, wide(xr[prev, 1]), wide(xr[after, 1]))
@@ -499,33 +510,31 @@
     for copy in load_cot:
         copy.wait()
     vertical_layers(adj_a, z1s, 4)
-    pl.semaphore_wait(barrier, 9)
-    vertical = send(z1s, z1r, partner)
-    for copy in load_flow:
-        copy.wait()
-    flow_moments(1)
-    vertical.wait_recv()
-    for which in range(2):
-        got = z1r[2 * which : 2 * which + 2]
-        phase[which, :2] = jnp.where(low, 0.0, got)
-        phase[which, 10:] = jnp.where(low, got, 0.0)
-    take_vertical(adj_a, z1r, 4)
-
-    first = []
+    pl.semaphore_wait(barrier, 13)
+    first = [send(z1s, z1r, partner)]
+
+    def edge_layer(values):
+        return jnp.where(low, values[7], values[0])
+
     for way in SIDES[2:]:
         slot = SLOT[way] - 2
         source = 0 if way[1] < 0 else 126
-        packed = jnp.where(
-            lanes_of(10) < 8,
-            roll(phase[1, 1:11], 6 - source, 2),
-            roll(phase[0, 1:11], 8 - source, 2),
+        middle = jnp.where(
+            lane3 < 8,
+            roll(phase[1, 2:10], 6 - source, 2),
+            roll(phase[0, 2:10], 8 - source, 2),
         )
-        y1s[slot, 0] = packed[0]
-        y1s[slot, 9] = packed[9]
-        middle = packed[1:9]
         entries = pack_y(adj_a, -way[1], None)
-        y1s[slot, 1:9] = jnp.where(lane3 < 6, entries, middle)
-        first.append(send(y1s.at[slot], y1r.at[slot], device(way)))
+        y1s[slot] = jnp.where(lane3 < 6, entries, middle)
+        first.append(send(y1s.at[slot], y1r.at[slot, pl.ds(1, 8)], device(way)))
+        rise, fall = slanted(-way[1], 2)
+        beyond = jnp.where(low, adj_a[fall, 8], adj_a[rise, 1])
+        edge = edge_layer(middle)
+        for i in (rise, fall):
+            k = ALONG_Y[-way[1]].index(i)
+            edge = jnp.where(lane == k, roll(beyond, k - (0 if way[1] < 0 else 127), 1), edge)
+        zy1s[slot] = edge
+        first.append(send(zy1s.at[slot], zy1r.at[slot], across(way)))
     for way in CORNERS:
         slot = SLOT[way]
         r = edge_row(-way[0])
@@ -540,12 +549,46 @@
         for n, which in enumerate((1, 0)):
             x1s[slot, 6 + 2 * n] = phase[which, 2:10, r, :]
             x1s[slot, 7 + 2 * n] = phase[which, 2:10, r + (1 if r == 0 else -1), :]
-            x1s[slot, 10, 2 * n : 2 * n + 1, :] = phase[which, 1, r : r + 1, :]
-            x1s[slot, 10, 2 * n + 1 : 2 * n + 2, :] = phase[which, 10, r : r + 1, :]
-        x1s[slot, 10, 4:, :] = jnp.zeros((4, 128), jnp.float32)
-        first.append(send(x1s.at[slot], x1r.at[slot], device(way)))
+            zx1s[slot, n : n + 1, :] = jnp.where(
+                low, phase[which, 9, r : r + 1, :], phase[which, 2, r : r + 1, :]
+            )
+        rise, fall = slanted(-way[0], 1)
+        zx1s[slot, 2:3, :] = jnp.where(
+            low, adj_a[fall, 8, r : r + 1, :], adj_a[rise, 1, r : r + 1, :]
+        )
+        zx1s[slot, 3:, :] = jnp.zeros((5, 128), jnp.float32)
+        first.append(send(x1s.at[slot], x1r.at[slot, pl.ds(0, 10)], device(way)))
+        first.append(send(zx1s.at[slot], zx1r.at[slot], across(way)))
+    for copy in load_flow:
+        copy.wait()
+    flow_moments(1)
     flow_moments(0)
     arrive(first)
+    for which in range(2):
+        got = z1r[2 * which : 2 * which + 2]
+        phase[which, :2] = jnp.where(low, 0.0, got)
+        phase[which, 10:] = jnp.where(low, got, 0.0)
+    take_vertical(adj_a, z1r, 4)
+    for way in SIDES:
+        sign = -way[0] - way[1]
+        if way[0]:
+            slot = SLOT[way]
+            rise, fall = slanted(sign, 1)
+            entry = zx1r[slot, 2:3, :]
+            x1r[slot, ALONG_X[sign].index(rise), 7:8, :] = entry
+            x1r[slot, ALONG_X[sign].index(fall), 0:1, :] = entry
+            for n in range(2):
+                line = zx1r[slot, n : n + 1, :]
+                x1r[slot, 10, 2 * n : 2 * n + 1, :] = jnp.where(low, 0.0, line)
+                x1r[slot, 10, 2 * n + 1 : 2 * n + 2, :] = jnp.where(low, line, 0.0)
+        else:
+            slot = SLOT[way] - 2
+            rise, fall = slanted(sign, 2)
+            tile = zy1r[slot]
+            y1r[slot, 0] = jnp.where(low, 0.0, tile)
+            y1r[slot, 9] = jnp.where(low, tile, 0.0)
+            y1r[slot, 8] = jnp.where(lane == ALONG_Y[sign].index(rise), tile, y1r[slot, 8])
+            y1r[slot, 1] = jnp.where(lane == ALONG_Y[sign].index(fall), tile, y1r[slot, 1])
     sources = (adj_a, x1r, y1r, 1, c1r, 2)
     phase_gradients(1, 6, 0)
     gather_flow(1, *sources)
@@ -554,9 +597,9 @@
     vertical_layers(adj_b, z2s, 0)
     vertical = send(z2s, z2r, partner)
     share = phase_share(1)
-    zcopy = send_share(share, zd2s, zd2r)
-    phase_gradients(0, 8, 2)
-    center, group = share_sides(share, zcopy, zd2r, xd2s, xd2r, yd2s, yd2r, cd2s, cd2r)
+    center, group = send_share(
+        share, zd2s, zd2r, zs2s, zs2r, xd2s, xd2r, yd2s, yd2r, cd2s, cd2r
+    )
     vertical.wait_recv()
     take_vertical(adj_b, z2r, 0)
     second = []
@@ -572,7 +615,8 @@
         slot = SLOT[way]
         rows_x(adj_b, -way[0], x2s, slot)
         second.append(send(x2s.at[slot], x2r.at[slot], device(way)))
-    phi[1:9] = collect_share(center, group, xd2r, yd2r, cd2r)
+    phase_gradients(0, 8, 2)
+    phi[1:9] = collect_share(center, group, zd2r, zs2r, xd2r, yd2r, cd2r)
     third = []
     for way in SIDES:
         slot = SLOT[way]
@@ -596,9 +640,10 @@
         load(out.at[pl.ds(10, 9)], out_hbm.at[pl.ds(10, 9)], 7),
     ]
     share = phase_share(0)
-    zcopy = send_share(share, zd4s, zd4r)
-    center, group = share_sides(share, zcopy, zd4r, xd4s, xd4r, yd4s, yd4r, cd4s, cd4r)
-    last = collect_share(center, group, xd4r, yd4r, cd4r)
+    center, group = send_share(
+        share, zd4s, zd4r, zs4s, zs4r, xd4s, xd4r, yd4s, yd4r, cd4s, cd4r
+    )
+    last = collect_share(center, group, zd4r, zs4r, xd4r, yd4r, cd4r)
     for k in range(7):
         out[19 + k] = out[19 + k] + last
     stores.append(load(out.at[pl.ds(19, 7)], out_hbm.at[pl.ds(19, 7)], 8))
@@ -613,7 +658,7 @@
         return pltpu.VMEM(shape + (8, 128), jnp.float32)
 
     share = [
-        vmem(4), vmem(4), vmem(2, 2), vmem(2, 2),
+        vmem(2), vmem(2), vmem(2), vmem(4), vmem(2, 2), vmem(2, 2),
         vmem(8), vmem(2, 8), vmem(2), vmem(4),
     ]
     scratch = [
@@ -622,13 +667,14 @@
         pltpu.VMEM(populations1.shape, populations1.dtype),
         vmem(26, 10), vmem(26, 10), vmem(2, 12), vmem(2, 6, 8), vmem(6, 8), vmem(8),
         vmem(2, 3, 10), vmem(10), vmem(2, 4, 8), vmem(11, 8), vmem(19, 8),
-        vmem(10), vmem(10), vmem(2, 11), vmem(2, 11), vmem(2, 10), vmem(2, 10), vmem(4, 3), vmem(4, 3),
+        vmem(10), vmem(10), vmem(2, 10), vmem(2, 11), vmem(2, 8), vmem(2, 10), vmem(4, 3), vmem(4, 3),
         vmem(6), vmem(6), vmem(2, 6), vmem(2, 6), vmem(2, 8), vmem(2, 8), vmem(4, 1), vmem(4, 1),
+        vmem(2), vmem(2), vmem(2), vmem(2),
         *share,
         vmem(), vmem(), vmem(2), vmem(2), vmem(2, 8),
         *share,
-        pltpu.SemaphoreType.DMA((48,)),
-        pltpu.SemaphoreType.DMA((48,)),
+        pltpu.SemaphoreType.DMA((64,)),
+        pltpu.SemaphoreType.DMA((64,)),
         pltpu.SemaphoreType.DMA((9,)),
     ]
     operands = [

time: 31.9 us -> 30.8 us (0.966)
  Pallas kernels: 30.8 us -> 29.8 us
    pallas_call x1, Pallas kernels: 30.8 us -> 29.8 us  [local(): pl.pallas_call(kernel, out_shape=jax.ShapeDtypeStruct(cotangent.shape, jn...]
where the time goes in v5:
time: 30.8 us; the launch traced here: 30.7 us
  Pallas kernels  29.8 us (97%)
  local copies, waits for them, and re-layouts  0.9 us (3%)
    pallas_call x1, Pallas kernels, local(): pl.pallas_call(kernel, out_shape=jax.ShapeDtypeStruct(cotangent.shape, jn...  29.8 us
    unnamed x1, local copies, waits for them, and re-layouts  0.9 us

profile of v5, /device:TPU:0, one launch (start us, length us, event | category | flops | bytes accessed | tf_op | source)
XLA Modules:
  0.0 30.7 jit_solution(13252063594742752828)
XLA Ops:
  0.0 29.8 %shard_map.37 = f32[26,8,8,128]{3,2,1,0:T(8,128)S(1)} custom-call(bf16[26,8,8,128]{3,2,1,0:T(8,128)(2,1)} %pop0_hbm.1, bf16[26,8,8,128]{3,2,1,0:T(8,128)(2,1)} %pop1_hbm.1, f32[26,8,8,128]{3,2,1,0:T(8,128)} %cot_hbm.1), custom_call_target="tpu_custom_call" | custom-call | tf_op jit(solution)/shard_map/pallas_call | solution.py:684
  29.8 0.9 %copy.5 = f32[26,8,8,128]{3,2,1,0:T(8,128)} copy(f32[26,8,8,128]{3,2,1,0:T(8,128)S(1)} %shard_map.37) | data formatting | bytes 1703936

commit v6 on v5

--- a/solution.py
+++ b/solution.py
@@ -35,6 +35,7 @@
 SHARPEN = 0.3
 PHASE_RATE = 1.4
 MESH = pl.DeviceIdType.MESH
+TOGETHER = 4
 
 RISING = [i for i in range(26) if VELOCITY[i][0] == 1]
 FALLING = [i for i in range(26) if VELOCITY[i][0] == -1]
@@ -276,6 +277,14 @@
     def dot(u, v):
         return u[0] * v[0] + u[1] * v[1] + u[2] * v[2]
 
+    def each_layer(layer):
+        def several(step, carry):
+            for n in range(TOGETHER):
+                layer(step * TOGETHER + n, carry)
+            return carry
+
+        lax.fori_loop(0, 8 // TOGETHER, several, 0)
+
     def flow_moments(which):
         def layer(z, carry):
             f = [pops[which][i, z].astype(jnp.float32) for i in range(19)]
@@ -284,7 +293,7 @@
                 flow[which, 1 + d, z] = signed(f, part(d))
             return carry
 
-        lax.fori_loop(0, 8, layer, 0)
+        each_layer(layer)
 
     def bounce(z, i, own, bounced):
         if VELOCITY[i][0] == 1:
@@ -334,7 +343,7 @@
             moments[10, z] = total([a[i] * pops[which][i, z].astype(jnp.float32) for i in range(19)])
             return carry
 
-        lax.fori_loop(0, 8, layer, 0)
+        each_layer(layer)
 
     def collide_adjoint(which, sources, result, offset, with_phi):
         def layer(z, carry):
@@ -419,7 +428,7 @@
                 result[19 + k, z + offset] = (1.0 - PHASE_RATE) * g[k]
             return carry
 
-        lax.fori_loop(0, 8, layer, 0)
+        each_layer(layer)
 
     def phase_share(which):
         def spread(first):

time: 30.8 us -> 29.7 us (0.964)
  Pallas kernels: 29.8 us -> 28.7 us
    pallas_call x1, Pallas kernels: 29.8 us -> 28.7 us  [local(): pl.pallas_call(kernel, out_shape=jax.ShapeDtypeStruct(cotangent.shape, jn...]
where the time goes in v6:
time: 29.7 us; the launch traced here: 29.6 us
  Pallas kernels  28.7 us (97%)
  local copies, waits for them, and re-layouts  0.9 us (3%)
    pallas_call x1, Pallas kernels, local(): pl.pallas_call(kernel, out_shape=jax.ShapeDtypeStruct(cotangent.shape, jn...  28.7 us
    unnamed x1, local copies, waits for them, and re-layouts  0.9 us

profile of v6, /device:TPU:0, one launch (start us, length us, event | category | flops | bytes accessed | tf_op | source)
XLA Modules:
  0.0 29.6 jit_solution(4744606127032145498)
XLA Ops:
  0.0 28.7 %shard_map.37 = f32[26,8,8,128]{3,2,1,0:T(8,128)S(1)} custom-call(bf16[26,8,8,128]{3,2,1,0:T(8,128)(2,1)} %pop0_hbm.1, bf16[26,8,8,128]{3,2,1,0:T(8,128)(2,1)} %pop1_hbm.1, f32[26,8,8,128]{3,2,1,0:T(8,128)} %cot_hbm.1), custom_call_target="tpu_custom_call" | custom-call | tf_op jit(solution)/shard_map/pallas_call | solution.py:693
  28.7 0.9 %copy.5 = f32[26,8,8,128]{3,2,1,0:T(8,128)} copy(f32[26,8,8,128]{3,2,1,0:T(8,128)S(1)} %shard_map.37) | data formatting | bytes 1703936

commit v7 on v6

--- a/solution.py
+++ b/solution.py
@@ -50,7 +50,7 @@
 
 def kernel(
     pop0_hbm, pop1_hbm, cot_hbm, out_hbm,
-    out, pop0, pop1, adj_a, adj_b, phase, grads, sens, phibar, slope, phi, flow, moments, arrive_f,
+    out, pop0, pop1, adj_a, adj_b, phase, grads, sens, phibar, slope, phi, flow, moments, arrive_f, pulls,
     z1s, z1r, x1s, x1r, y1s, y1r, c1s, c1r,
     z2s, z2r, x2s, x2r, y2s, y2r, c2s, c2r,
     zx1s, zx1r, zy1s, zy1r,
@@ -414,8 +414,20 @@
                 sens[d, z] = pull * (b1[d] - normal[d] * nb1)
                 sens[3 + d, z] = -frac * fbar[d]
             phibar[z] = frac_bar
-            pbar = rate * a0
-            keep = 1.0 - rate
+            for d in range(3):
+                pulls[d, z] = jbar[d]
+            pulls[3, z] = rate * a0
+            for k in range(7):
+                result[19 + k, z + offset] = (1.0 - PHASE_RATE) * g[k]
+            return carry
+
+        each_layer(layer)
+
+    def flow_result(which, result, offset):
+        def layer(z, carry):
+            keep = -0.1 - 0.5 * phase[which, z + 2]
+            jbar = [pulls[d, z] for d in range(3)]
+            pbar = pulls[3, z]
             for i in range(19):
                 value = keep * arrive_f[i, z] + pbar
                 for d in range(3):
@@ -424,8 +436,6 @@
                     elif VELOCITY[i][d] == -1:
                         value = value - jbar[d]
                 result[i, z + offset] = value
-            for k in range(7):
-                result[19 + k, z + offset] = (1.0 - PHASE_RATE) * g[k]
             return carry
 
         each_layer(layer)
@@ -603,12 +613,14 @@
     gather_flow(1, *sources)
     collide_adjoint(1, sources, adj_b, 1, False)
 
-    vertical_layers(adj_b, z2s, 0)
-    vertical = send(z2s, z2r, partner)
     share = phase_share(1)
     center, group = send_share(
         share, zd2s, zd2r, zs2s, zs2r, xd2s, xd2r, yd2s, yd2r, cd2s, cd2r
     )
+    flow_result(1, adj_b, 1)
+    vertical_layers(adj_b, z2s, 0)
+    vertical = send(z2s, z2r, partner)
+    phase_gradients(0, 8, 2)
     vertical.wait_recv()
     take_vertical(adj_b, z2r, 0)
     second = []
@@ -624,7 +636,6 @@
         slot = SLOT[way]
         rows_x(adj_b, -way[0], x2s, slot)
         second.append(send(x2s.at[slot], x2r.at[slot], device(way)))
-    phase_gradients(0, 8, 2)
     phi[1:9] = collect_share(center, group, zd2r, zs2r, xd2r, yd2r, cd2r)
     third = []
     for way in SIDES:
@@ -644,14 +655,15 @@
     phi[9] = z3r[...]
     collide_adjoint(0, sources, out, 0, True)
 
+    share = phase_share(0)
+    center, group = send_share(
+        share, zd4s, zd4r, zs4s, zs4r, xd4s, xd4r, yd4s, yd4r, cd4s, cd4r
+    )
+    flow_result(0, out, 0)
     stores = [
         load(out.at[pl.ds(0, 10)], out_hbm.at[pl.ds(0, 10)], 6),
         load(out.at[pl.ds(10, 9)], out_hbm.at[pl.ds(10, 9)], 7),
     ]
-    share = phase_share(0)
-    center, group = send_share(
-        share, zd4s, zd4r, zs4s, zs4r, xd4s, xd4r, yd4s, yd4r, cd4s, cd4r
-    )
     last = collect_share(center, group, zd4r, zs4r, xd4r, yd4r, cd4r)
     for k in range(7):
         out[19 + k] = out[19 + k] + last
@@ -675,7 +687,7 @@
         pltpu.VMEM(populations0.shape, populations0.dtype),
         pltpu.VMEM(populations1.shape, populations1.dtype),
         vmem(26, 10), vmem(26, 10), vmem(2, 12), vmem(2, 6, 8), vmem(6, 8), vmem(8),
-        vmem(2, 3, 10), vmem(10), vmem(2, 4, 8), vmem(11, 8), vmem(19, 8),
+        vmem(2, 3, 10), vmem(10), vmem(2, 4, 8), vmem(11, 8), vmem(19, 8), vmem(4, 8),
         vmem(10), vmem(10), vmem(2, 10), vmem(2, 11), vmem(2, 8), vmem(2, 10), vmem(4, 3), vmem(4, 3),
         vmem(6), vmem(6), vmem(2, 6), vmem(2, 6), vmem(2, 8), vmem(2, 8), vmem(4, 1), vmem(4, 1),
         vmem(2), vmem(2), vmem(2), vmem(2),

time: 29.7 us -> 29.1 us (0.980)
  Pallas kernels: 28.7 us -> 28.1 us
    pallas_call x1, Pallas kernels: 28.7 us -> 28.1 us  [local(): pl.pallas_call(kernel, out_shape=jax.ShapeDtypeStruct(cotangent.shape, jn...]
where the time goes in v7:
time: 29.1 us; the launch traced here: 29 us
  Pallas kernels  28.1 us (97%)
  local copies, waits for them, and re-layouts  0.9 us (3%)
    pallas_call x1, Pallas kernels, local(): pl.pallas_call(kernel, out_shape=jax.ShapeDtypeStruct(cotangent.shape, jn...  28.1 us
    unnamed x1, local copies, waits for them, and re-layouts  0.9 us

profile of v7, /device:TPU:0, one launch (start us, length us, event | category | flops | bytes accessed | tf_op | source)
XLA Modules:
  0.0 29.0 jit_solution(12961625010242885817)
XLA Ops:
  0.0 28.1 %shard_map.37 = f32[26,8,8,128]{3,2,1,0:T(8,128)S(1)} custom-call(bf16[26,8,8,128]{3,2,1,0:T(8,128)(2,1)} %pop0_hbm.1, bf16[26,8,8,128]{3,2,1,0:T(8,128)(2,1)} %pop1_hbm.1, f32[26,8,8,128]{3,2,1,0:T(8,128)} %cot_hbm.1), custom_call_target="tpu_custom_call" | custom-call | tf_op jit(solution)/shard_map/pallas_call | solution.py:705
  28.1 0.9 %copy.5 = f32[26,8,8,128]{3,2,1,0:T(8,128)} copy(f32[26,8,8,128]{3,2,1,0:T(8,128)S(1)} %shard_map.37) | data formatting | bytes 1703936
